TPU v7x, 32 devices: a whole 2x2x4 slice. The times are simulated.
32 devices in a mesh: grp: 2 (over x), seq: 16 (over z, y, core).
Axes of the slice: x: 2, y: 2, z: 4, core: 2. Of those that a mesh axis runs over, the one named last changes fastest.
Arguments:
- queries: bfloat16 [24576, 1024], P(('grp', 'seq')), parts along dimension 0, may hold values from -16 to 16
- key_states: bfloat16 [24576, 1024], P(('grp', 'seq')), parts along dimension 0, may hold values from -8 to 8
- values: bfloat16 [24576, 1024], P(('grp', 'seq')), parts along dimension 0, may hold values from -6 to 6
- grad_out: bfloat16 [24576, 1024], P(('grp', 'seq')), parts along dimension 0, may hold values from -6 to 6
- tile_pairs: int32 [192, 5], P('grp'), parts along dimension 0, may hold values from 0 to 95, as said below
- counts: int32 [192], P('grp'), parts along dimension 0, may hold values from 1 to 5
Outputs:
- grad_queries: bfloat16 [24576, 1024], P(('grp', 'seq')), parts along dimension 0
- grad_keys: bfloat16 [24576, 1024], P(('grp', 'seq')), parts along dimension 0
- grad_values: bfloat16 [24576, 1024], P(('grp', 'seq')), parts along dimension 0
There are 2 independent parts, one for each index of `grp`. A program takes and returns all parts, laid end to end along the dimension named above; each array names one. Nothing has to cross between parts.
Inputs may be any that keep to these rules, and one draw needn't show every extreme that they name: `tile_pairs`: slot 0 of query tile t holds t itself; the first counts[t] slots hold distinct tiles within 2 tiles of t; the remaining slots hold tiles within that reach and are not attended.
All inputs are finite; a program needn't handle non-finite values.
Results may differ from a plain program's by a relative error of at most 0.0066.
Values may be sent and summed in bfloat16 or wider, within the bound.
No kernel may reach another device: no remote copies, remote signals or barrier semaphores. Data moves between devices by JAX's collectives and lax.ppermute only.
A program may use at most 128 MiB of HBM per device.

v0:
```python
import functools

import jax
import jax.numpy as jnp
from jax import lax
from jax.experimental import pallas as pl
from jax.experimental.pallas import tpu as pltpu
from jax.sharding import PartitionSpec as P

HEAD_DIM = 64
SCALE = HEAD_DIM ** (-0.5)
SCALE_LOG2 = SCALE * 1.4426950408889634
REACH = 2
BAND = 2 * REACH + 1
TILE = 128
BLOCK = REACH * TILE
PAIR = 2 * HEAD_DIM
DEAD = 1e30
CHUNKS = 2
GROUP = 4
F32 = jnp.float32
BF16 = jnp.bfloat16
NT = (((1,), (1,)), ((), ()))
VMEM_BYTES = 60 * 1024 * 1024
KEYS = 3 * BLOCK
KEY_TILES = KEYS // TILE


def merge(*sequences):
    items = []
    for place, sequence in enumerate(sequences):
        for at, emit in enumerate(sequence):
            items.append(((at + 0.5) / len(sequence), place, emit))
    items.sort(key=lambda item: item[:2])
    for _, _, emit in items:
        emit()


def by_head(x):
    first_head = lax.broadcasted_iota(jnp.int32, x.shape, 1) < HEAD_DIM
    zero = jnp.zeros_like(x)
    return jnp.concatenate([jnp.where(first_head, x, zero), jnp.where(first_head, zero, x)], axis=0)


def fill_dead(tile, pairs, counts, dead):
    for n in range(REACH):
        live = counts[tile + n]
        for o in range(BAND):
            hit = jnp.int32(0)
            for s in range(pairs.shape[1]):
                same = (pairs[tile + n, s] == tile + n + o - REACH) & (s < live)
                hit = hit | same.astype(jnp.int32)
            dead[n, o] = jnp.where(hit > 0, 0.0, DEAD)


def attend(pairs_here, q, do, dq, k_ext, v_ext, kt, dk_acc, dv_acc, dead, bufs):
    qw, dw, s_buf, dp_buf, p_buf, ds_buf = bufs
    units = [(g, n) for g in range(pairs_here) for n in range(REACH)]
    half = 32
    state = {}

    def at(u):
        g, n = units[u]
        lanes = slice(g * PAIR, (g + 1) * PAIR)
        return g, n, lanes, slice(n * TILE, (n + 1) * TILE), slice(n * TILE, (n + BAND) * TILE)

    def scores(u):
        g, n, lanes, rows, band = at(u)
        b, w = u % 2, u % 3

        def weights():
            qw[w] = by_head(q[rows, lanes])
            dw[w] = by_head(do[rows, lanes])

        def product():
            state[u, "s"] = lax.dot_general(
                k_ext[band, lanes], qw[w], NT, preferred_element_type=F32
            )

        def one(o):
            def emit():
                here = slice(o * TILE, (o + 1) * TILE)
                s = state[u, "s"][here]
                s_buf[b, here] = s
                top = jnp.max(s.reshape(TILE // 8, 8, 2 * TILE), axis=0) - dead[n, o]
                state[u, "m"] = top if o == 0 else jnp.maximum(state[u, "m"], top)

            return emit

        def grad_probs():
            dp_buf[b] = lax.dot_general(v_ext[band, lanes], dw[w], NT, preferred_element_type=F32)

        return [weights, product] + [one(o) for o in range(BAND)] + [grad_probs]

    def softmax(u):
        n, b = units[u][1], u % 2

        def parts(o):
            return [slice(o * TILE + c, o * TILE + c + half) for c in range(0, TILE, half)]

        def fold(x):
            return jnp.sum(x.reshape(half // 8, 8, 2 * TILE), axis=0)

        def peak():
            state[u, "m"] = jnp.max(state[u, "m"], axis=0, keepdims=True) * SCALE_LOG2
            state[u, "l"] = jnp.zeros((8, 2 * TILE), F32)
            state[u, "d"] = jnp.zeros((8, 2 * TILE), F32)

        def powers(o):
            def emit():
                shift = state[u, "m"] + dead[n, o]
                for r in parts(o):
                    e = jnp.exp2(s_buf[b, r] * SCALE_LOG2 - shift)
                    s_buf[b, r] = e
                    state[u, "l"] = state[u, "l"] + fold(e)

            return emit

        def total():
            state[u, "r"] = 1.0 / jnp.sum(state[u, "l"], axis=0, keepdims=True)

        def normal(o):
            def emit():
                for r in parts(o):
                    p = s_buf[b, r] * state[u, "r"]
                    s_buf[b, r] = p
                    p_buf[b, r] = p.astype(BF16)
                    state[u, "d"] = state[u, "d"] + fold(p * dp_buf[b, r])

            return emit

        def delta():
            state[u, "d"] = jnp.sum(state[u, "d"], axis=0, keepdims=True)

        def score_grads(o):
            def emit():
                for r in parts(o):
                    ds_buf[b, r] = (s_buf[b, r] * (dp_buf[b, r] - state[u, "d"])).astype(BF16)

            return emit

        out = [peak] + [powers(o) for o in range(BAND)]
        out += [total] + [normal(o) for o in range(BAND)]
        return out + [delta] + [score_grads(o) for o in range(BAND)]

    def grads(u):
        g, n, lanes, rows, band = at(u)
        b, w = u % 2, u % 3

        def keyed(source, weight, acc):
            def emit():
                x = jnp.dot(source[b], weight[w], preferred_element_type=F32)
                if n == 0:
                    acc[band, lanes] = x
                else:
                    shared = slice(n * TILE, BAND * TILE)
                    acc[shared, lanes] = acc[shared, lanes] + x[: (BAND - n) * TILE]
                    acc[BAND * TILE :, lanes] = x[(BAND - n) * TILE :]

            return emit

        def query():
            x = jnp.dot(kt[g, :, band], ds_buf[b], preferred_element_type=F32)
            first_head = lax.broadcasted_iota(jnp.int32, (PAIR, TILE), 0) < HEAD_DIM
            dq[rows, lanes] = (
                jnp.where(first_head, x[:, :TILE], x[:, TILE:]).T * SCALE
            ).astype(BF16)

        return [keyed(p_buf, dw, dv_acc), query, keyed(ds_buf, qw, dk_acc)]

    count = len(units)
    for step in range(count + 2):
        merge(
            scores(step) if step < count else [],
            softmax(step - 1) if 0 <= step - 1 < count else [],
            grads(step - 2) if 0 <= step - 2 < count else [],
        )


def scratch(group):
    lanes, band = group * PAIR, BAND * TILE
    return [
        pltpu.VMEM((KEYS, lanes), BF16),
        pltpu.VMEM((KEYS, lanes), BF16),
        pltpu.VMEM((group, PAIR, KEYS), BF16),
        pltpu.VMEM((KEYS, lanes), F32),
        pltpu.VMEM((KEYS, lanes), F32),
        pltpu.SMEM((REACH, BAND), F32),
        pltpu.VMEM((3, 2 * TILE, PAIR), BF16),
        pltpu.VMEM((3, 2 * TILE, PAIR), BF16),
        pltpu.VMEM((2, band, 2 * TILE), F32),
        pltpu.VMEM((2, band, 2 * TILE), F32),
        pltpu.VMEM((2, band, 2 * TILE), BF16),
        pltpu.VMEM((2, band, 2 * TILE), BF16),
    ]


def transpose_keys(group, k_ext, kt):
    for g in range(group):
        for j in range(KEY_TILES):
            rows = slice(j * TILE, (j + 1) * TILE)
            kt[g, :, rows] = k_ext[rows, g * PAIR : (g + 1) * PAIR].T


def edge_kernel(group, chained, place, pairs, counts, q, do, k_near, k_mid, v_near, v_mid, halo, *rest):
    rest = rest[1:] if chained else rest
    dq, part_k, part_v, send, k_ext, v_ext, kt, dk_acc, dv_acc, dead, *bufs = rest
    low_edge = place[1] == 0
    outside = pl.multiple_of(jnp.where(low_edge, 0, 2 * BLOCK), BLOCK)
    inside = pl.multiple_of(jnp.where(low_edge, 2 * BLOCK, 0), BLOCK)

    @pl.when(pl.program_id(0) == 0)
    def _():
        fill_dead(place[0] + place[1] * REACH, pairs, counts, dead)

    for row, near, mid, ext in ((0, k_near, k_mid, k_ext), (BLOCK, v_near, v_mid, v_ext)):
        ext[pl.ds(outside, BLOCK)] = halo[row : row + BLOCK]
        ext[BLOCK : 2 * BLOCK] = near[...]
        ext[pl.ds(inside, BLOCK)] = mid[...]
    transpose_keys(group, k_ext, kt)
    attend(group, q, do, dq, k_ext, v_ext, kt, dk_acc, dv_acc, dead, bufs)
    for acc, part, row, scale in ((dk_acc, part_k, 0, SCALE), (dv_acc, part_v, BLOCK, 1.0)):
        send[row : row + BLOCK] = (acc[pl.ds(outside, BLOCK)] * scale).astype(BF16)
        part[:BLOCK] = acc[BLOCK : 2 * BLOCK]
        part[BLOCK:] = acc[pl.ds(inside, BLOCK)]


def inner_kernel(
    group, place, pairs, counts, q, do, k, v, chip_k, chip_v, cross_k, cross_v, back, dq_in, *rest
):
    dq, dk, dv, k_ext, v_ext, kt, dk_acc, dv_acc, dead, *bufs = rest
    cross = pl.multiple_of(place[1] * BLOCK, BLOCK)
    chip = pl.multiple_of(2 * BLOCK - cross, BLOCK)

    @pl.when(pl.program_id(0) == 0)
    def _():
        fill_dead(place[0] + REACH, pairs, counts, dead)

    transpose_keys(group, k, kt)
    attend(group, q, do, dq, k, v, kt, dk_acc, dv_acc, dead, bufs)
    for acc, part, other, row, out, scale in (
        (dk_acc, chip_k, cross_k, 0, dk, SCALE),
        (dv_acc, chip_v, cross_v, BLOCK, dv, 1.0),
    ):
        out[pl.ds(cross, BLOCK)] = ((acc[pl.ds(cross, BLOCK)] + other[:BLOCK]) * scale).astype(BF16)
        middle = acc[BLOCK : 2 * BLOCK] + part[BLOCK:] + other[BLOCK:]
        out[BLOCK : 2 * BLOCK] = (middle * scale).astype(BF16)
        edge = (acc[pl.ds(chip, BLOCK)] + part[:BLOCK]) * scale
        out[pl.ds(chip, BLOCK)] = (edge + back[row : row + BLOCK].astype(F32)).astype(BF16)


def join_kernel(place, dk, dv, back, dk_out, dv_out):
    dk_out[...] = (dk[...].astype(F32) + back[:BLOCK].astype(F32)).astype(BF16)
    dv_out[...] = (dv[...].astype(F32) + back[BLOCK:].astype(F32)).astype(BF16)


def shards(queries, key_states, values, grad_out, tile_pairs, counts):
    rows_dev, width = queries.shape
    tiles_dev = rows_dev // TILE
    n_seq = lax.axis_size("seq")
    me = lax.axis_index("seq")
    chip_swap = [(i, i ^ 1) for i in range(n_seq) if i ^ 1 < n_seq]
    cross_swap = [(i, i + 1) for i in range(1, n_seq - 1, 2)]
    cross_swap = cross_swap + [(b, a) for a, b in cross_swap]
    first = me * tiles_dev
    cross_block = jnp.where(me % 2 == 0, 0, 2)
    cross_place = jnp.stack([first, cross_block]).astype(jnp.int32)
    chip_place = jnp.stack([first, 2 - cross_block]).astype(jnp.int32)
    span = width // CHUNKS
    params = pltpu.CompilerParams(vmem_limit_bytes=VMEM_BYTES)
    cost = pl.CostEstimate(flops=1, bytes_accessed=1, transcendentals=0)

    def pack(block, columns):
        return jnp.concatenate(
            [
                lax.dynamic_slice_in_dim(x[:, columns], block * BLOCK, BLOCK, 0)
                for x in (key_states, values)
            ],
            axis=0,
        )

    chunks = [slice(c * span, (c + 1) * span) for c in range(CHUNKS)]
    chip_halo = lax.ppermute(pack(2 - cross_block, slice(0, width)), "seq", chip_swap)
    cross_halos = [lax.ppermute(pack(cross_block, c), "seq", cross_swap) for c in chunks]

    def edge(place, halo, column, lanes, dq):
        group = min(GROUP, lanes // PAIR)
        wide = group * PAIR
        at = column // wide

        def near(h, place, *_):
            return (place[1], at + h)

        def mid(h, *_):
            return (1, at + h)

        def own(h, *_):
            return (0, h)

        one = pl.BlockSpec((BLOCK, wide), near)
        two = pl.BlockSpec((BLOCK, wide), mid)
        double = pl.BlockSpec((2 * BLOCK, wide), own)
        operands = [place, tile_pairs, counts, queries, grad_out, key_states, key_states]
        operands += [values, values, halo]
        aliases = {}
        if dq is not None:
            aliases = {len(operands): 0}
            operands.append(dq)
        return pl.pallas_call(
            functools.partial(edge_kernel, group, dq is not None),
            grid_spec=pltpu.PrefetchScalarGridSpec(
                num_scalar_prefetch=3,
                grid=(lanes // wide,),
                in_specs=[one, one, one, two, one, two, double]
                + [pl.BlockSpec(memory_space=pl.ANY)] * len(aliases),
                out_specs=[one, double, double, double],
                scratch_shapes=scratch(group),
            ),
            out_shape=[
                jax.ShapeDtypeStruct((rows_dev, width), BF16),
                jax.ShapeDtypeStruct((2 * BLOCK, lanes), F32),
                jax.ShapeDtypeStruct((2 * BLOCK, lanes), F32),
                jax.ShapeDtypeStruct((2 * BLOCK, lanes), BF16),
            ],
            input_output_aliases=aliases,
            compiler_params=params,
            cost_estimate=cost,
            name="edge_tiles",
        )(*operands)

    dq, chip_k, chip_v, chip_send = edge(chip_place, chip_halo, 0, width, None)
    chip_back = lax.ppermute(chip_send, "seq", chip_swap)
    parts_k, parts_v, cross_back = [], [], []
    for c, halo in zip(chunks, cross_halos):
        dq, part_k, part_v, send = edge(cross_place, halo, c.start, span, dq)
        parts_k.append(part_k)
        parts_v.append(part_v)
        cross_back.append(lax.ppermute(send, "seq", cross_swap))

    wide = min(GROUP, span // PAIR) * PAIR
    grad_keys = grad_values = None
    for c, part_k, part_v in zip(chunks, parts_k, parts_v):
        at = c.start // wide

        def spec(rows, row, column):
            return pl.BlockSpec((rows, wide), lambda h, *_, row=row, column=column: (row, column + h))

        operands = [cross_place, tile_pairs, counts, queries, grad_out, key_states, values]
        operands += [chip_k, chip_v, part_k, part_v, chip_back, dq]
        aliases = {len(operands) - 1: 0}
        chained = []
        if grad_keys is not None:
            aliases |= {len(operands): 1, len(operands) + 1: 2}
            chained = [grad_keys, grad_values]

        def kernel(*refs, skip=len(chained)):
            head = len(operands)
            inner_kernel(wide // PAIR, *refs[:head], *refs[head + skip :])

        dq, grad_keys, grad_values = pl.pallas_call(
            kernel,
            grid_spec=pltpu.PrefetchScalarGridSpec(
                num_scalar_prefetch=3,
                grid=(span // wide,),
                in_specs=[spec(BLOCK, 1, at)] * 2
                + [spec(KEYS, 0, at)] * 2
                + [spec(2 * BLOCK, 0, at)] * 2
                + [spec(2 * BLOCK, 0, 0)] * 2
                + [spec(2 * BLOCK, 0, at)]
                + [pl.BlockSpec(memory_space=pl.ANY)] * (1 + len(chained)),
                out_specs=[spec(BLOCK, 1, at), spec(KEYS, 0, at), spec(KEYS, 0, at)],
                scratch_shapes=scratch(wide // PAIR),
            ),
            out_shape=[jax.ShapeDtypeStruct((rows_dev, width), BF16)] * 3,
            input_output_aliases=aliases,
            compiler_params=params,
            cost_estimate=cost,
            name="inner_tiles",
        )(*operands, *chained)

    for c, back in zip(chunks, cross_back):

        def edge_block(h, place, at=c.start // span):
            return (place[1], at)

        spec = pl.BlockSpec((BLOCK, span), edge_block)
        grad_keys, grad_values = pl.pallas_call(
            join_kernel,
            grid_spec=pltpu.PrefetchScalarGridSpec(
                num_scalar_prefetch=1,
                grid=(1,),
                in_specs=[spec, spec, pl.BlockSpec((2 * BLOCK, span), lambda h, *_: (0, 0))],
                out_specs=[spec, spec],
            ),
            out_shape=[jax.ShapeDtypeStruct((rows_dev, width), BF16)] * 2,
            input_output_aliases={1: 0, 2: 1},
            compiler_params=params,
            cost_estimate=cost,
            name="join_edges",
        )(cross_place, grad_keys, grad_values, back)
    return (dq, grad_keys, grad_values)


def solution(mesh):
    rows = P(("grp", "seq"), None)
    return jax.shard_map(
        shards,
        mesh=mesh,
        in_specs=(rows, rows, rows, rows, P("grp", None), P("grp")),
        out_specs=(rows, rows, rows),
        check_vma=False,
    )
```

profile of v0, /device:TPU:13, one launch (start us, length us, event | category | flops | bytes accessed | tf_op | source)
XLA Modules:
  0.0 86.9 jit_solution(16927229787153150455)
XLA Ops:
  0.6 1.3 %constant_dynamic-slice_fusion.4 = (bf16[256,1024]{1,0:T(8,128)(2,1)S(1)}, bf16[256,1024]{1,0:T(8,128)(2,1)S(1)}) fusion(bf16[768,1024]{1,0:T(8,128)(2,1)} %refs_6_.3, s32[]{:T(128)S(6)} %select_n.23, bf16[768,1024]{1,0:T(8,128)(2,1)} %refs_5_.3), kind=kLoop, calls=%fused_computation.7 | loop fusion | bytes 2097156 | tf_op jit(solution)/shard_map/dynamic_slice | solution.py:276
  1.9 1.0 %pad_maximum_fusion = bf16[512,1024]{1,0:T(8,128)(2,1)} fusion(bf16[256,1024]{1,0:T(8,128)(2,1)S(1)} %get-tuple-element.51, bf16[256,1024]{1,0:T(8,128)(2,1)S(1)} %get-tuple-element.52), kind=kLoop, calls=%fused_computation | loop fusion | flops 2097152 | bytes 2097152 | tf_op jit(solution)/shard_map/concatenate | solution.py:274
  3.0 0.7 collective-permute-start
  3.7 1.0 %fusion = (bf16[768,512]{1,0:T(8,128)(2,1)S(1)}, bf16[768,512]{1,0:T(8,128)(2,1)}) fusion(bf16[768,1024]{1,0:T(8,128)(2,1)S(1)} %copy-done), kind=kLoop, calls=%fused_computation.11 | loop fusion | bytes 3145728 | tf_op jit(solution)/shard_map/slice | solution.py:276
  4.7 0.7 copy-done.1
  5.6 3.7 %collective-permute-start.2 = (bf16[512,512]{1,0:T(8,128)(2,1)S(1)}, bf16[512,512]{1,0:T(8,128)(2,1)S(1)}, u32[]{:S(2)}, u32[]{:S(2)}) collective-permute-start(bf16[512,512]{1,0:T(8,128)(2,1)S(1)} %pad_maximum_fusion.2), channel_id=1, source_target_pairs={{1,2},{3,4},{5,6},{7,8},{9,10},{11,12},{13,14},{2,1},{4,3},{6,5},{... | collective-permute-start | bytes 1572872 | tf_op jit(solution)/shard_map/ppermute | solution.py:284
  9.4 0.7 copy.23.pairs.refs_1_
  10.1 0.6 pad_add_fusion.1.place
  10.7 1.0 %constant_dynamic-slice_fusion.2 = (bf16[256,512]{1,0:T(8,128)(2,1)S(1)}, bf16[256,512]{1,0:T(8,128)(2,1)S(1)}) fusion(bf16[768,512]{1,0:T(8,128)(2,1)S(1)} %get-tuple-element.50, s32[]{:T(128)S(6)} %select_n.24, bf16[768,512]{1,0:T(8,128)(2,1)} %get-tuple-element.48), kind=kLoop, calls=%fused_computation.5 | loop fusion | bytes 1048580 | tf_op jit(solution)/shard_map/dynamic_slice | solution.py:276
  11.7 14.7 %edge_tiles.3 = (bf16[768,1024]{1,0:T(8,128)(2,1)}, f32[512,1024]{1,0:T(8,128)}, f32[512,1024]{1,0:T(8,128)}, bf16[512,1024]{1,0:T(8,128)(2,1)}) custom-call(s32[2]{0:T(128)} %pad_add_fusion.1.place, s32[96,5]{1,0:T(8,128)} %copy.23.pairs.refs_1_, s32[96]{0:T(128)} %refs_2_.3, bf16[768,1024]{1,0:T(8,128)(2,1)} %refs_3_.3, bf16[768,1024]{1,0:T(8,128)(2,1)} %refs_4_.3, ...), custom_call_target="tpu_custom_call" | custom-call | flops 1 | bytes 1 | tf_op jit(solution)/shard_map/edge_tiles/pallas_call | solution.py:309
  26.5 3.5 %collective-permute-start.1 = (bf16[512,512]{1,0:T(8,128)(2,1)S(1)}, bf16[512,512]{1,0:T(8,128)(2,1)S(1)}, u32[]{:S(2)}, u32[]{:S(2)}) collective-permute-start(bf16[512,512]{1,0:T(8,128)(2,1)S(1)} %pad_maximum_fusion.1), channel_id=1, source_target_pairs={{1,2},{3,4},{5,6},{7,8},{9,10},{11,12},{13,14},{2,1},{4,3},{6,5},{... | collective-permute-start | bytes 1572872 | tf_op jit(solution)/shard_map/ppermute | solution.py:284
  30.6 0.8 copy-done.3
  31.4 9.6 %edge_tiles.4 = (bf16[768,1024]{1,0:T(8,128)(2,1)}, f32[512,512]{1,0:T(8,128)}, f32[512,512]{1,0:T(8,128)}, bf16[512,512]{1,0:T(8,128)(2,1)}) custom-call(s32[2]{0:T(128)} %pad_add_fusion.place.refs_0_, s32[96,5]{1,0:T(8,128)} %copy.23.pairs.refs_1_, s32[96]{0:T(128)} %refs_2_.3, bf16[768,1024]{1,0:T(8,128)(2,1)} %refs_3_.3, ...), custom_call_target="tpu_custom_call", output_to_operand_aliasing={{0}: (10, {})} | custom-call | flops 1 | bytes 1 | tf_op jit(solution)/shard_map/edge_tiles/pallas_call | solution.py:309
  41.0 3.1 %collective-permute-start.4 = (bf16[512,512]{1,0:T(8,128)(2,1)}, bf16[512,512]{1,0:T(8,128)(2,1)S(1)}, u32[]{:S(2)}, u32[]{:S(2)}) collective-permute-start(bf16[512,512]{1,0:T(8,128)(2,1)} %get-tuple-element.41), channel_id=1, source_target_pairs={{1,2},{3,4},{5,6},{7,8},{9,10},{11,12},{13,14},{2,1},{4,3},{6,5},{... | collective-permute-start | bytes 1572872 | tf_op jit(solution)/shard_map/ppermute | solution.py:338
  44.1 0.8 copy-done.4
  44.9 9.6 %edge_tiles.5 = (bf16[768,1024]{1,0:T(8,128)(2,1)}, f32[512,512]{1,0:T(8,128)}, f32[512,512]{1,0:T(8,128)}, bf16[512,512]{1,0:T(8,128)(2,1)}) custom-call(s32[2]{0:T(128)} %pad_add_fusion.place.refs_0_, s32[96,5]{1,0:T(8,128)} %copy.23.pairs.refs_1_, s32[96]{0:T(128)} %refs_2_.3, bf16[768,1024]{1,0:T(8,128)(2,1)} %refs_3_.3, ...), custom_call_target="tpu_custom_call", output_to_operand_aliasing={{0}: (10, {})} | custom-call | flops 1 | bytes 1 | tf_op jit(solution)/shard_map/edge_tiles/pallas_call | solution.py:309
  54.5 3.5 %collective-permute-start.5 = (bf16[512,512]{1,0:T(8,128)(2,1)}, bf16[512,512]{1,0:T(8,128)(2,1)S(1)}, u32[]{:S(2)}, u32[]{:S(2)}) collective-permute-start(bf16[512,512]{1,0:T(8,128)(2,1)} %get-tuple-element.44), channel_id=1, source_target_pairs={{1,2},{3,4},{5,6},{7,8},{9,10},{11,12},{13,14},{2,1},{4,3},{6,5},{... | collective-permute-start | bytes 1572872 | tf_op jit(solution)/shard_map/ppermute | solution.py:338
  58.0 1.0 %copy-done.2 = bf16[512,1024]{1,0:T(8,128)(2,1)} copy-done((bf16[512,1024]{1,0:T(8,128)(2,1)}, bf16[512,1024]{1,0:T(8,128)(2,1)S(1)}, u32[]{:S(2)}) %copy-start.2) | copy-done | bytes 1048600
  59.0 10.4 %inner_tiles.2 = (bf16[768,1024]{1,0:T(8,128)(2,1)}, bf16[768,1024]{1,0:T(8,128)(2,1)}, bf16[768,1024]{1,0:T(8,128)(2,1)}) custom-call(s32[2]{0:T(128)} %pad_add_fusion.place.refs_0_, s32[96,5]{1,0:T(8,128)} %copy.23.pairs.refs_1_, s32[96]{0:T(128)} %refs_2_.3, bf16[768,1024]{1,0:T(8,128)(2,1)} %refs_3_.3, ...), custom_call_target="tpu_custom_call", output_to_operand_aliasing={{0}: (12, {})} | custom-call | flops 1 | bytes 1 | tf_op jit(solution)/shard_map/inner_tiles/pallas_call | solution.py:360
  69.4 10.4 %inner_tiles.3 = (bf16[768,1024]{1,0:T(8,128)(2,1)}, bf16[768,1024]{1,0:T(8,128)(2,1)}, bf16[768,1024]{1,0:T(8,128)(2,1)}) custom-call(s32[2]{0:T(128)} %pad_add_fusion.place.refs_0_, s32[96,5]{1,0:T(8,128)} %copy.23.pairs.refs_1_, s32[96]{0:T(128)} %refs_2_.3, ...), custom_call_target="tpu_custom_call", output_to_operand_aliasing={{0}: (12, {}), {1}: (13, {}), {2}: (14, {})} | custom-call | flops 1 | bytes 1 | tf_op jit(solution)/shard_map/inner_tiles/pallas_call | solution.py:360
  79.8 0.8 copy-done.5
  80.6 2.7 %join_edges.2 = (bf16[768,1024]{1,0:T(8,128)(2,1)}, bf16[768,1024]{1,0:T(8,128)(2,1)}) custom-call(s32[2]{0:T(128)} %pad_add_fusion.place.refs_0_, bf16[768,1024]{1,0:T(8,128)(2,1)} %get-tuple-element.39.dk, bf16[768,1024]{1,0:T(8,128)(2,1)} %get-tuple-element.40.dv, bf16[512,512]{1,0:T(8,128)(2,1)} %copy-done.5), custom_call_target="tpu_custom_call", output_to_operand_aliasing={{0}: (1, {}), {1}: (2, {})} | custom-call | flops 1 | bytes 1 | tf_op jit(solution)/shard_map/join_edges/pallas_call | solution.py:387
  83.4 0.8 copy-done.6
  84.2 2.7 %join_edges.3 = (bf16[768,1024]{1,0:T(8,128)(2,1)}, bf16[768,1024]{1,0:T(8,128)(2,1)}) custom-call(s32[2]{0:T(128)} %pad_add_fusion.place.refs_0_, bf16[768,1024]{1,0:T(8,128)(2,1)} %get-tuple-element.42.dk, bf16[768,1024]{1,0:T(8,128)(2,1)} %get-tuple-element.43.dv, bf16[512,512]{1,0:T(8,128)(2,1)} %copy-done.6), custom_call_target="tpu_custom_call", output_to_operand_aliasing={{0}: (1, {}), {1}: (2, {})} | custom-call | flops 1 | bytes 1 | tf_op jit(solution)/shard_map/join_edges/pallas_call | solution.py:387
  (22 shorter events, 1.0 us)
Async XLA Ops:
  1.9 1.8 %copy-start = (bf16[768,1024]{1,0:T(8,128)(2,1)S(1)}, bf16[768,1024]{1,0:T(8,128)(2,1)}, u32[]{:S(2)}) copy-start(bf16[768,1024]{1,0:T(8,128)(2,1)} %refs_5_.3) | copy-start | bytes 4718596
  3.0 8.7 %collective-permute-start = (bf16[512,1024]{1,0:T(8,128)(2,1)}, bf16[512,1024]{1,0:T(8,128)(2,1)}, u32[]{:S(2)}, u32[]{:S(2)}) collective-permute-start(bf16[512,1024]{1,0:T(8,128)(2,1)} %pad_maximum_fusion), channel_id=1, source_target_pairs={{0,1},{1,0},{2,3},{3,2},{4,5},{5,4},{6,7},{7,6},{8,9},{9,8},{10,11... | collective-permute-start | bytes 3145736 | tf_op jit(solution)/shard_map/ppermute | solution.py:283
  3.7 1.7 %copy-start.1 = (bf16[768,1024]{1,0:T(8,128)(2,1)S(1)}, bf16[768,1024]{1,0:T(8,128)(2,1)}, u32[]{:S(2)}) copy-start(bf16[768,1024]{1,0:T(8,128)(2,1)} %refs_6_.3) | copy-start | bytes 4718596
  5.5 3.8 %copy-start.7 = (s32[96,5]{0,1:T(8,128)S(1)}, s32[96,5]{0,1:T(8,128)}, u32[]{:S(2)}) copy-start(s32[96,5]{0,1:T(8,128)} %param.10) | copy-start | bytes 5764
  5.6 25.0 %collective-permute-start.2 = (bf16[512,512]{1,0:T(8,128)(2,1)S(1)}, bf16[512,512]{1,0:T(8,128)(2,1)S(1)}, u32[]{:S(2)}, u32[]{:S(2)}) collective-permute-start(bf16[512,512]{1,0:T(8,128)(2,1)S(1)} %pad_maximum_fusion.2), channel_id=1, source_target_pairs={{1,2},{3,4},{5,6},{7,8},{9,10},{11,12},{13,14},{2,1},{4,3},{6,5},{... | collective-permute-start | bytes 1572872 | tf_op jit(solution)/shard_map/ppermute | solution.py:284
  26.4 31.6 %collective-permute-start.3 = (bf16[512,1024]{1,0:T(8,128)(2,1)}, bf16[512,1024]{1,0:T(8,128)(2,1)S(1)}, u32[]{:S(2)}, u32[]{:S(2)}) collective-permute-start(bf16[512,1024]{1,0:T(8,128)(2,1)} %get-tuple-element.31), channel_id=1, source_target_pairs={{0,1},{1,0},{2,3},{3,2},{4,5},{5,4},{6,7},{7,6},{8,9},{9,8},{10,11... | collective-permute-start | bytes 3145736 | tf_op jit(solution)/shard_map/ppermute | solution.py:332
  26.5 17.6 %collective-permute-start.1 = (bf16[512,512]{1,0:T(8,128)(2,1)S(1)}, bf16[512,512]{1,0:T(8,128)(2,1)S(1)}, u32[]{:S(2)}, u32[]{:S(2)}) collective-permute-start(bf16[512,512]{1,0:T(8,128)(2,1)S(1)} %pad_maximum_fusion.1), channel_id=1, source_target_pairs={{1,2},{3,4},{5,6},{7,8},{9,10},{11,12},{13,14},{2,1},{4,3},{6,5},{... | collective-permute-start | bytes 1572872 | tf_op jit(solution)/shard_map/ppermute | solution.py:284
  30.6 0.8 copy-start.3
  41.0 38.9 %collective-permute-start.4 = (bf16[512,512]{1,0:T(8,128)(2,1)}, bf16[512,512]{1,0:T(8,128)(2,1)S(1)}, u32[]{:S(2)}, u32[]{:S(2)}) collective-permute-start(bf16[512,512]{1,0:T(8,128)(2,1)} %get-tuple-element.41), channel_id=1, source_target_pairs={{1,2},{3,4},{5,6},{7,8},{9,10},{11,12},{13,14},{2,1},{4,3},{6,5},{... | collective-permute-start | bytes 1572872 | tf_op jit(solution)/shard_map/ppermute | solution.py:338
  44.1 0.8 copy-start.4
  54.5 28.9 %collective-permute-start.5 = (bf16[512,512]{1,0:T(8,128)(2,1)}, bf16[512,512]{1,0:T(8,128)(2,1)S(1)}, u32[]{:S(2)}, u32[]{:S(2)}) collective-permute-start(bf16[512,512]{1,0:T(8,128)(2,1)} %get-tuple-element.44), channel_id=1, source_target_pairs={{1,2},{3,4},{5,6},{7,8},{9,10},{11,12},{13,14},{2,1},{4,3},{6,5},{... | collective-permute-start | bytes 1572872 | tf_op jit(solution)/shard_map/ppermute | solution.py:338
  58.0 1.0 %copy-start.2 = (bf16[512,1024]{1,0:T(8,128)(2,1)}, bf16[512,1024]{1,0:T(8,128)(2,1)S(1)}, u32[]{:S(2)}) copy-start(bf16[512,1024]{1,0:T(8,128)(2,1)S(1)} %collective-permute-done.3.refs_11_) | copy-start | bytes 3145732
  79.8 0.8 copy-start.5
  83.4 0.8 copy-start.6
where the time goes:
time: 87.9 us; the launch traced here: 86.9 us
  Pallas kernels  60.1 us (68%)
  starting transfers between devices  14.6 us (17%)
  local copies, waits for them, and re-layouts  9.05 us (10%)
  other arithmetic  2.27 us (3%)
    pallas_call x3, Pallas kernels, edge(): pl.pallas_call(functools.partial(edge_kernel, group, dq is not None), gri...  33.9 us
    pallas_call x2, Pallas kernels, shards(): pl.pallas_call(kernel, grid_spec=pltpu.PrefetchScalarGridSpec(num_scalar_...  20.8 us
    ppermute x2, starting transfers between devices, shards(): lax.ppermute(pack(cross_block, c), 'seq', cross_swap)  7.24 us
    ppermute x2, starting transfers between devices, shards(): cross_back.append(lax.ppermute(send, 'seq', cross_swap))  6.61 us
    unnamed x17, local copies, waits for them, and re-layouts  5.65 us
    pallas_call x2, Pallas kernels, shards(): pl.pallas_call(join_kernel, grid_spec=pltpu.PrefetchScalarGridSpec(num_sc...  5.43 us
    dynamic_slice x3, local copies, waits for them, and re-layouts, pack(): lax.dynamic_slice_in_dim(x[:, columns], block * BLOCK, BLOCK, 0)  2.3 us
  transfers between devices with their start and end apart: 6, of which 0 were waited for; matrix products, arithmetic and copies ran while one was open for 5% of the time, Pallas kernels for 66%

commit v1 on v0

v1 whole, which is shorter than its diff:
```python
import functools

import jax
import jax.numpy as jnp
from jax import lax
from jax.experimental import pallas as pl
from jax.experimental.pallas import tpu as pltpu
from jax.sharding import PartitionSpec as P

HEAD_DIM = 64
SCALE = HEAD_DIM ** (-0.5)
SCALE_LOG2 = SCALE * 1.4426950408889634
REACH = 2
BAND = 2 * REACH + 1
TILE = 128
BLOCK = REACH * TILE
PAIR = 2 * HEAD_DIM
DEAD = 1e30
CHUNKS = 2
GROUP = 2
F32 = jnp.float32
BF16 = jnp.bfloat16
NT = (((1,), (1,)), ((), ()))
VMEM_BYTES = 63 * 1024 * 1024 + 768 * 1024
KEYS = 3 * BLOCK
KEY_TILES = KEYS // TILE


def merge(*sequences):
    items = []
    for place, sequence in enumerate(sequences):
        for at, emit in enumerate(sequence):
            items.append(((at + 0.5) / len(sequence), place, emit))
    items.sort(key=lambda item: item[:2])
    for _, _, emit in items:
        emit()


def by_head(x):
    first_head = lax.broadcasted_iota(jnp.int32, x.shape, 1) < HEAD_DIM
    zero = jnp.zeros_like(x)
    return jnp.concatenate([jnp.where(first_head, x, zero), jnp.where(first_head, zero, x)], axis=0)


def dead_slots(first, tiles_dev, tile_pairs, counts):
    chosen = lax.dynamic_slice_in_dim(tile_pairs, first, tiles_dev, 0)
    live = lax.dynamic_slice_in_dim(counts, first, tiles_dev, 0)
    own = first + jnp.arange(tiles_dev, dtype=jnp.int32)
    offset = jnp.arange(BAND, dtype=jnp.int32) - REACH
    slot = jnp.arange(tile_pairs.shape[1], dtype=jnp.int32)
    same = chosen[:, None, :] == (own[:, None] + offset[None, :])[:, :, None]
    hit = jnp.any(same & (slot[None, None, :] < live[:, None, None]), axis=2)
    return jnp.where(hit, 0.0, DEAD).astype(F32)


def attend(pairs_here, base, q, do, dq, k_ext, v_ext, kt, dk_acc, dv_acc, dead, bufs):
    qw, dw, s_buf, dp_buf, p_buf, ds_buf = bufs
    units = [(g, n) for g in range(pairs_here) for n in range(REACH)]
    half = 32
    state = {}

    def at(u):
        g, n = units[u]
        lanes = slice(g * PAIR, (g + 1) * PAIR)
        return g, n, lanes, slice(n * TILE, (n + 1) * TILE), slice(n * TILE, (n + BAND) * TILE)

    def scores(u):
        g, n, lanes, rows, band = at(u)
        b, w = u % 2, u % 3

        def weights():
            qw[w] = by_head(q[rows, lanes])
            dw[w] = by_head(do[rows, lanes])

        def product():
            state[u, "s"] = lax.dot_general(
                k_ext[band, lanes], qw[w], NT, preferred_element_type=F32
            )

        def one(o):
            def emit():
                here = slice(o * TILE, (o + 1) * TILE)
                s = state[u, "s"][here]
                s_buf[b, here] = s
                top = jnp.max(s.reshape(TILE // 8, 8, 2 * TILE), axis=0) - dead[base + n, o]
                state[u, "m"] = top if o == 0 else jnp.maximum(state[u, "m"], top)

            return emit

        def grad_probs():
            dp_buf[b] = lax.dot_general(v_ext[band, lanes], dw[w], NT, preferred_element_type=F32)

        return [weights, product] + [one(o) for o in range(BAND)] + [grad_probs]

    def softmax(u):
        n, b = units[u][1], u % 2

        def parts(o):
            return [slice(o * TILE + c, o * TILE + c + half) for c in range(0, TILE, half)]

        def fold(x):
            return jnp.sum(x.reshape(half // 8, 8, 2 * TILE), axis=0)

        def peak():
            state[u, "m"] = jnp.max(state[u, "m"], axis=0, keepdims=True) * SCALE_LOG2
            state[u, "l"] = jnp.zeros((8, 2 * TILE), F32)
            state[u, "d"] = jnp.zeros((8, 2 * TILE), F32)

        def powers(o):
            def emit():
                shift = state[u, "m"] + dead[base + n, o]
                for r in parts(o):
                    e = jnp.exp2(s_buf[b, r] * SCALE_LOG2 - shift)
                    s_buf[b, r] = e
                    state[u, "l"] = state[u, "l"] + fold(e)

            return emit

        def total():
            state[u, "r"] = 1.0 / jnp.sum(state[u, "l"], axis=0, keepdims=True)

        def normal(o):
            def emit():
                for r in parts(o):
                    p = s_buf[b, r] * state[u, "r"]
                    s_buf[b, r] = p
                    p_buf[b, r] = p.astype(BF16)
                    state[u, "d"] = state[u, "d"] + fold(p * dp_buf[b, r])

            return emit

        def delta():
            state[u, "d"] = jnp.sum(state[u, "d"], axis=0, keepdims=True)

        def score_grads(o):
            def emit():
                for r in parts(o):
                    ds_buf[b, r] = (s_buf[b, r] * (dp_buf[b, r] - state[u, "d"])).astype(BF16)

            return emit

        out = [peak] + [powers(o) for o in range(BAND)]
        out += [total] + [normal(o) for o in range(BAND)]
        return out + [delta] + [score_grads(o) for o in range(BAND)]

    def grads(u):
        g, n, lanes, rows, band = at(u)
        b, w = u % 2, u % 3

        def keyed(source, weight, acc):
            def emit():
                x = jnp.dot(source[b], weight[w], preferred_element_type=F32)
                if n == 0:
                    acc[band, lanes] = x
                else:
                    shared = slice(n * TILE, BAND * TILE)
                    acc[shared, lanes] = acc[shared, lanes] + x[: (BAND - n) * TILE]
                    acc[BAND * TILE :, lanes] = x[(BAND - n) * TILE :]

            return emit

        def query():
            x = jnp.dot(kt[g, :, band], ds_buf[b], preferred_element_type=F32)
            first_head = lax.broadcasted_iota(jnp.int32, (PAIR, TILE), 0) < HEAD_DIM
            dq[rows, lanes] = (
                jnp.where(first_head, x[:, :TILE], x[:, TILE:]).T * SCALE
            ).astype(BF16)

        return [keyed(p_buf, dw, dv_acc), query, keyed(ds_buf, qw, dk_acc)]

    count = len(units)
    for step in range(count + 2):
        merge(
            scores(step) if step < count else [],
            softmax(step - 1) if 0 <= step - 1 < count else [],
            grads(step - 2) if 0 <= step - 2 < count else [],
        )


def scratch(group):
    lanes, band = group * PAIR, BAND * TILE
    return [
        pltpu.VMEM((KEYS, lanes), BF16),
        pltpu.VMEM((KEYS, lanes), BF16),
        pltpu.VMEM((group, PAIR, KEYS), BF16),
        pltpu.VMEM((KEYS, lanes), F32),
        pltpu.VMEM((KEYS, lanes), F32),
        pltpu.VMEM((3, 2 * TILE, PAIR), BF16),
        pltpu.VMEM((3, 2 * TILE, PAIR), BF16),
        pltpu.VMEM((2, band, 2 * TILE), F32),
        pltpu.VMEM((2, band, 2 * TILE), F32),
        pltpu.VMEM((2, band, 2 * TILE), BF16),
        pltpu.VMEM((2, band, 2 * TILE), BF16),
    ]


def transpose_keys(group, k_ext, kt):
    for g in range(group):
        for j in range(KEY_TILES):
            rows = slice(j * TILE, (j + 1) * TILE)
            kt[g, :, rows] = k_ext[rows, g * PAIR : (g + 1) * PAIR].T


def edge_kernel(group, chained, place, dead, q, do, k_near, k_mid, v_near, v_mid, halo, *rest):
    rest = rest[chained:]
    dq, part_k, part_v, send, k_ext, v_ext, kt, dk_acc, dv_acc, *bufs = rest
    low_edge = place[0] == 0
    outside = pl.multiple_of(jnp.where(low_edge, 0, 2 * BLOCK), BLOCK)
    inside = pl.multiple_of(jnp.where(low_edge, 2 * BLOCK, 0), BLOCK)

    for row, near, mid, ext in ((0, k_near, k_mid, k_ext), (BLOCK, v_near, v_mid, v_ext)):
        ext[pl.ds(outside, BLOCK)] = halo[row : row + BLOCK]
        ext[BLOCK : 2 * BLOCK] = near[...]
        ext[pl.ds(inside, BLOCK)] = mid[...]
    transpose_keys(group, k_ext, kt)
    attend(group, place[0] * REACH, q, do, dq, k_ext, v_ext, kt, dk_acc, dv_acc, dead, bufs)
    for acc, part, row, scale in ((dk_acc, part_k, 0, SCALE), (dv_acc, part_v, BLOCK, 1.0)):
        send[row : row + BLOCK] = (acc[pl.ds(outside, BLOCK)] * scale).astype(BF16)
        part[:BLOCK] = acc[BLOCK : 2 * BLOCK]
        part[BLOCK:] = acc[pl.ds(inside, BLOCK)]


def inner_kernel(
    group, place, dead, q, do, k, v, chip_k, chip_v, cross_k, cross_v, back, dq_in, *rest
):
    dq, dk, dv, kt, dk_acc, dv_acc, *bufs = rest
    cross = pl.multiple_of(place[0] * BLOCK, BLOCK)
    chip = pl.multiple_of(2 * BLOCK - cross, BLOCK)

    transpose_keys(group, k, kt)
    attend(group, REACH, q, do, dq, k, v, kt, dk_acc, dv_acc, dead, bufs)
    for acc, part, other, row, out, scale in (
        (dk_acc, chip_k, cross_k, 0, dk, SCALE),
        (dv_acc, chip_v, cross_v, BLOCK, dv, 1.0),
    ):
        out[pl.ds(cross, BLOCK)] = ((acc[pl.ds(cross, BLOCK)] + other[:BLOCK]) * scale).astype(BF16)
        middle = acc[BLOCK : 2 * BLOCK] + part[BLOCK:] + other[BLOCK:]
        out[BLOCK : 2 * BLOCK] = (middle * scale).astype(BF16)
        edge = (acc[pl.ds(chip, BLOCK)] + part[:BLOCK]) * scale
        out[pl.ds(chip, BLOCK)] = (edge + back[row : row + BLOCK].astype(F32)).astype(BF16)


def join_kernel(place, dk, dv, *rest):
    *backs, dk_out, dv_out = rest
    span = backs[0].shape[1]
    for c, back in enumerate(backs):
        lanes = slice(c * span, (c + 1) * span)
        dk_out[:, lanes] = (dk[:, lanes].astype(F32) + back[:BLOCK].astype(F32)).astype(BF16)
        dv_out[:, lanes] = (dv[:, lanes].astype(F32) + back[BLOCK:].astype(F32)).astype(BF16)


def shards(queries, key_states, values, grad_out, tile_pairs, counts):
    rows_dev, width = queries.shape
    tiles_dev = rows_dev // TILE
    n_seq = lax.axis_size("seq")
    me = lax.axis_index("seq")
    chip_swap = [(i, i ^ 1) for i in range(n_seq) if i ^ 1 < n_seq]
    cross_swap = [(i, i + 1) for i in range(1, n_seq - 1, 2)]
    cross_swap = cross_swap + [(b, a) for a, b in cross_swap]
    first = me * tiles_dev
    cross_block = jnp.where(me % 2 == 0, 0, 2)
    cross_place = jnp.reshape(cross_block, (1,)).astype(jnp.int32)
    chip_place = jnp.reshape(2 - cross_block, (1,)).astype(jnp.int32)
    dead = dead_slots(first, tiles_dev, tile_pairs, counts)
    span = width // CHUNKS
    params = pltpu.CompilerParams(vmem_limit_bytes=VMEM_BYTES)
    cost = pl.CostEstimate(flops=1, bytes_accessed=1, transcendentals=0)

    def pack(block, columns):
        return jnp.concatenate(
            [
                lax.dynamic_slice_in_dim(x[:, columns], block * BLOCK, BLOCK, 0)
                for x in (key_states, values)
            ],
            axis=0,
        )

    chunks = [slice(c * span, (c + 1) * span) for c in range(CHUNKS)]
    cross_out = pack(cross_block, slice(0, width))
    cross_halo = lax.ppermute(cross_out, "seq", cross_swap)
    chip_halo = lax.ppermute(pack(2 - cross_block, slice(0, width)), "seq", chip_swap)

    def edge(place, halo, column, lanes, earlier):
        group = min(GROUP, lanes // PAIR)
        wide = group * PAIR
        at = column // wide

        def near(h, place, *_):
            return (place[0], at + h)

        def mid(h, *_):
            return (1, at + h)

        def own(h, *_):
            return (0, h)

        one = pl.BlockSpec((BLOCK, wide), near)
        two = pl.BlockSpec((BLOCK, wide), mid)
        double = pl.BlockSpec((2 * BLOCK, wide), own)
        halo_block = pl.BlockSpec((2 * BLOCK, wide), lambda h, *_: (0, at + h))
        operands = [place, dead, queries, grad_out, key_states, key_states]
        operands += [values, values, halo]
        aliases = {}
        for i, array in enumerate(earlier):
            if array is not None:
                aliases[len(operands)] = i
                operands.append(array)
        return pl.pallas_call(
            functools.partial(edge_kernel, group, len(aliases)),
            grid_spec=pltpu.PrefetchScalarGridSpec(
                num_scalar_prefetch=2,
                grid=(lanes // wide,),
                in_specs=[one, one, one, two, one, two, halo_block]
                + [pl.BlockSpec(memory_space=pl.ANY)] * len(aliases),
                out_specs=[one, halo_block, halo_block, double],
                scratch_shapes=scratch(group),
            ),
            out_shape=[
                jax.ShapeDtypeStruct((rows_dev, width), BF16),
                jax.ShapeDtypeStruct((2 * BLOCK, width), F32),
                jax.ShapeDtypeStruct((2 * BLOCK, width), F32),
                jax.ShapeDtypeStruct((2 * BLOCK, lanes), BF16),
            ],
            input_output_aliases=aliases,
            compiler_params=params,
            cost_estimate=cost,
            name="edge_tiles",
        )(*operands)

    dq, chip_k, chip_v, chip_send = edge(chip_place, chip_halo, 0, width, [None] * 3)
    chip_back = lax.ppermute(chip_send, "seq", chip_swap)
    cross_k = cross_v = None
    cross_back = []
    for c in chunks:
        dq, cross_k, cross_v, send = edge(
            cross_place, cross_halo, c.start, span, [dq, cross_k, cross_v]
        )
        cross_back.append(lax.ppermute(send, "seq", cross_swap))

    wide = GROUP * PAIR

    def spec(rows, row):
        return pl.BlockSpec((rows, wide), lambda h, *_: (row, h))

    operands = [cross_place, dead, queries, grad_out, key_states, values]
    operands += [chip_k, chip_v, cross_k, cross_v, chip_back, dq]
    dq, grad_keys, grad_values = pl.pallas_call(
        functools.partial(inner_kernel, GROUP),
        grid_spec=pltpu.PrefetchScalarGridSpec(
            num_scalar_prefetch=2,
            grid=(width // wide,),
            in_specs=[spec(BLOCK, 1)] * 2
            + [spec(KEYS, 0)] * 2
            + [spec(2 * BLOCK, 0)] * 5
            + [pl.BlockSpec(memory_space=pl.ANY)],
            out_specs=[spec(BLOCK, 1), spec(KEYS, 0), spec(KEYS, 0)],
            scratch_shapes=scratch(GROUP)[2:],
        ),
        out_shape=[jax.ShapeDtypeStruct((rows_dev, width), BF16)] * 3,
        input_output_aliases={len(operands) - 1: 0},
        compiler_params=params,
        cost_estimate=cost,
        name="inner_tiles",
    )(*operands)

    edge_spec = pl.BlockSpec((BLOCK, width), lambda h, place: (place[0], 0))
    grad_keys, grad_values = pl.pallas_call(
        join_kernel,
        grid_spec=pltpu.PrefetchScalarGridSpec(
            num_scalar_prefetch=1,
            grid=(1,),
            in_specs=[edge_spec] * 2
            + [pl.BlockSpec((2 * BLOCK, span), lambda h, *_: (0, 0))] * CHUNKS,
            out_specs=[edge_spec] * 2,
        ),
        out_shape=[jax.ShapeDtypeStruct((rows_dev, width), BF16)] * 2,
        input_output_aliases={1: 0, 2: 1},
        compiler_params=params,
        cost_estimate=cost,
        name="join_edges",
    )(cross_place, grad_keys, grad_values, *cross_back)
    return (dq, grad_keys, grad_values)


def solution(mesh):
    rows = P(("grp", "seq"), None)
    return jax.shard_map(
        shards,
        mesh=mesh,
        in_specs=(rows, rows, rows, rows, P("grp", None), P("grp")),
        out_specs=(rows, rows, rows),
        check_vma=False,
    )
```

time: 87.9 us -> 72.5 us (0.82)
  the two profiles are of different devices: /device:TPU:13 before, /device:TPU:17 now
where the time goes in v1:
time: 72.5 us; the launch traced here: 71.9 us
  Pallas kernels  48.3 us (67%)
  starting transfers between devices  9.83 us (14%)
  waiting for transfers between devices  8.79 us (12%)
  other arithmetic  2.12 us (3%)
  local copies, waits for them, and re-layouts  2.1 us (3%)
  between operations  0.75 us (1%)
    pallas_call x3, Pallas kernels, edge(): pl.pallas_call(functools.partial(edge_kernel, group, len(aliases)), grid_...  31 us
    pallas_call x1, Pallas kernels, shards(): pl.pallas_call(functools.partial(inner_kernel, GROUP), grid_spec=pltpu.Pr...  14.5 us
    ppermute x1, waiting for transfers between devices, shards(): cross_halo = lax.ppermute(cross_out, 'seq', cross_swap)  8.78 us
    ppermute x2, starting transfers between devices, shards(): cross_back.append(lax.ppermute(send, 'seq', cross_swap))  5.56 us
    ppermute x1, starting transfers between devices, shards(): cross_halo = lax.ppermute(cross_out, 'seq', cross_swap)  3.04 us
    pallas_call x1, Pallas kernels, shards(): pl.pallas_call(join_kernel, grid_spec=pltpu.PrefetchScalarGridSpec(num_sc...  2.67 us
    dynamic_slice x1, local copies, waits for them, and re-layouts, pack(): lax.dynamic_slice_in_dim(x[:, columns], block * BLOCK, BLOCK, 0)  1.74 us
  transfers between devices with their start and end apart: 5, of which 1 were waited for; matrix products, arithmetic and copies ran while one was open for 3% of the time, Pallas kernels for 63%

profile of v1, /device:TPU:17, one launch (start us, length us, event | category | flops | bytes accessed | tf_op | source)
XLA Modules:
  0.0 71.9 jit_solution(12655884166487371823)
XLA Ops:
  0.6 0.0 copy-start
  0.7 1.7 %constant_dynamic-slice_fusion = (bf16[256,1024]{1,0:T(8,128)(2,1)S(1)}, bf16[256,1024]{1,0:T(8,128)(2,1)S(1)}, bf16[256,1024]{1,0:T(8,128)(2,1)S(1)}, bf16[256,1024]{1,0:T(8,128)(2,1)S(1)}) fusion(bf16[768,1024]{1,0:T(8,128)(2,1)} %v.1, s32[]{:T(128)S(6)} %select_n.32, s32[]{:T(128)S(6)} %select_n.31, bf16[768,1024]{1,0:T(8,128)(2,1)} %k.1), kind=kLoop, calls=%fused_computation.6 | loop fusion | bytes 4194312 | tf_op jit(solution)/shard_map/dynamic_slice | solution.py:272
  2.4 0.1 pad_maximum_fusion
  2.5 0.0 copy-start.1
  2.5 0.7 %collective-permute-start = (bf16[512,1024]{1,0:T(8,128)(2,1)S(1)}, bf16[512,1024]{1,0:T(8,128)(2,1)}, u32[]{:S(2)}, u32[]{:S(2)}) collective-permute-start(bf16[512,1024]{1,0:T(8,128)(2,1)S(1)} %pad_maximum_fusion), channel_id=1, source_target_pairs={{0,1},{1,0},{2,3},{3,2},{4,5},{5,4},{6,7},{7,6},{8,9},{9,8},{10,11... | collective-permute-start | bytes 3145736 | tf_op jit(solution)/shard_map/ppermute | solution.py:281
  3.2 1.0 %pad_maximum_fusion.1 = bf16[512,1024]{1,0:T(8,128)(2,1)} fusion(bf16[256,1024]{1,0:T(8,128)(2,1)S(1)} %get-tuple-element.39, bf16[256,1024]{1,0:T(8,128)(2,1)S(1)} %get-tuple-element.42), kind=kLoop, calls=%fused_computation.1 | loop fusion | flops 2097152 | bytes 2097152 | tf_op jit(solution)/shard_map/concatenate | solution.py:270
  4.3 3.0 %collective-permute-start.1 = (bf16[512,1024]{1,0:T(8,128)(2,1)}, bf16[512,1024]{1,0:T(8,128)(2,1)}, u32[]{:S(2)}, u32[]{:S(2)}) collective-permute-start(bf16[512,1024]{1,0:T(8,128)(2,1)} %pad_maximum_fusion.1), channel_id=1, source_target_pairs={{1,2},{3,4},{5,6},{7,8},{9,10},{11,12},{13,14},{2,1},{4,3},{6,5},{... | collective-permute-start | bytes 3145736 | tf_op jit(solution)/shard_map/ppermute | solution.py:280
  7.3 0.1 constant_dynamic-slice_fusion.4
  7.4 0.1 dynamic_slice.19
  7.5 0.1 copy.17
  7.6 0.1 broadcast_add_fusion
  7.7 0.1 iota_compare_fusion
  7.7 0.3 and_reduce_fusion
  8.0 0.1 copy.18
  8.1 0.6 broadcast_select_fusion.dead
  8.7 13.9 %edge_tiles.3 = (bf16[768,1024]{1,0:T(8,128)(2,1)}, f32[512,1024]{1,0:T(8,128)}, f32[512,1024]{1,0:T(8,128)}, bf16[512,1024]{1,0:T(8,128)(2,1)}) custom-call(s32[1]{0:T(128)} %bitcast.1.place, f32[6,5]{1,0:T(8,128)} %broadcast_select_fusion.dead, bf16[768,1024]{1,0:T(8,128)(2,1)} %q.7, bf16[768,1024]{1,0:T(8,128)(2,1)} %do.7, bf16[768,1024]{1,0:T(8,128)(2,1)} %k.1, ...), custom_call_target="tpu_custom_call" | custom-call | flops 1 | bytes 1 | tf_op jit(solution)/shard_map/edge_tiles/pallas_call | solution.py:308
  22.7 0.5 collective-permute-start.2
  23.2 8.8 %collective-permute-done.1.halo = bf16[512,1024]{1,0:T(8,128)(2,1)} collective-permute-done((bf16[512,1024]{1,0:T(8,128)(2,1)}, bf16[512,1024]{1,0:T(8,128)(2,1)}, u32[]{:S(2)}, u32[]{:S(2)}) %collective-permute-start.1) | collective-permute-done | bytes 1048608 | tf_op jit(solution)/shard_map/ppermute | solution.py:280
  31.9 8.5 %edge_tiles.4 = (bf16[768,1024]{1,0:T(8,128)(2,1)}, f32[512,1024]{1,0:T(8,128)}, f32[512,1024]{1,0:T(8,128)}, bf16[512,512]{1,0:T(8,128)(2,1)}) custom-call(s32[1]{0:T(128)} %bitcast.place, f32[6,5]{1,0:T(8,128)} %broadcast_select_fusion.dead, bf16[768,1024]{1,0:T(8,128)(2,1)} %q.7, bf16[768,1024]{1,0:T(8,128)(2,1)} %do.7, ...), custom_call_target="tpu_custom_call", output_to_operand_aliasing={{0}: (9, {})} | custom-call | flops 1 | bytes 1 | tf_op jit(solution)/shard_map/edge_tiles/pallas_call | solution.py:308
  40.5 8.6 %edge_tiles.5 = (bf16[768,1024]{1,0:T(8,128)(2,1)}, f32[512,1024]{1,0:T(8,128)}, f32[512,1024]{1,0:T(8,128)}, bf16[512,512]{1,0:T(8,128)(2,1)}) custom-call(s32[1]{0:T(128)} %bitcast.place, f32[6,5]{1,0:T(8,128)} %broadcast_select_fusion.dead, bf16[768,1024]{1,0:T(8,128)(2,1)} %q.7, ...), custom_call_target="tpu_custom_call", output_to_operand_aliasing={{0}: (9, {}), {1}: (10, {}), {2}: (11, {})} | custom-call | flops 1 | bytes 1 | tf_op jit(solution)/shard_map/edge_tiles/pallas_call | solution.py:308
  49.0 3.0 %collective-permute-start.4 = (bf16[512,512]{1,0:T(8,128)(2,1)}, bf16[512,512]{1,0:T(8,128)(2,1)}, u32[]{:S(2)}, u32[]{:S(2)}) collective-permute-start(bf16[512,512]{1,0:T(8,128)(2,1)} %get-tuple-element.34), channel_id=1, source_target_pairs={{1,2},{3,4},{5,6},{7,8},{9,10},{11,12},{13,14},{2,1},{4,3},{6,5},{... | collective-permute-start | bytes 1572872 | tf_op jit(solution)/shard_map/ppermute | solution.py:338
  52.0 2.6 %collective-permute-start.3 = (bf16[512,512]{1,0:T(8,128)(2,1)}, bf16[512,512]{1,0:T(8,128)(2,1)}, u32[]{:S(2)}, u32[]{:S(2)}) collective-permute-start(bf16[512,512]{1,0:T(8,128)(2,1)} %get-tuple-element.33), channel_id=1, source_target_pairs={{1,2},{3,4},{5,6},{7,8},{9,10},{11,12},{13,14},{2,1},{4,3},{6,5},{... | collective-permute-start | bytes 1572872 | tf_op jit(solution)/shard_map/ppermute | solution.py:338
  54.6 14.5 %inner_tiles.1 = (bf16[768,1024]{1,0:T(8,128)(2,1)}, bf16[768,1024]{1,0:T(8,128)(2,1)}, bf16[768,1024]{1,0:T(8,128)(2,1)}) custom-call(s32[1]{0:T(128)} %bitcast.place, f32[6,5]{1,0:T(8,128)} %broadcast_select_fusion.dead, bf16[768,1024]{1,0:T(8,128)(2,1)} %q.7, bf16[768,1024]{1,0:T(8,128)(2,1)} %do.7, ...), custom_call_target="tpu_custom_call", output_to_operand_aliasing={{0}: (11, {})} | custom-call | flops 1 | bytes 1 | tf_op jit(solution)/shard_map/inner_tiles/pallas_call | solution.py:347
  69.2 2.7 %join_edges.1 = (bf16[768,1024]{1,0:T(8,128)(2,1)}, bf16[768,1024]{1,0:T(8,128)(2,1)}) custom-call(s32[1]{0:T(128)} %bitcast.place, bf16[768,1024]{1,0:T(8,128)(2,1)} %get-tuple-element.31.dk, bf16[768,1024]{1,0:T(8,128)(2,1)} %get-tuple-element.32.dv, ...), custom_call_target="tpu_custom_call", output_to_operand_aliasing={{0}: (1, {}), {1}: (2, {})} | custom-call | flops 1 | bytes 1 | tf_op jit(solution)/shard_map/join_edges/pallas_call | solution.py:367
  (8 shorter events, 0.0 us)
Async XLA Ops:
  0.6 6.7 %copy-start = (s32[96,5]{0,1:T(8,128)S(1)}, s32[96,5]{0,1:T(8,128)}, u32[]{:S(2)}) copy-start(s32[96,5]{0,1:T(8,128)} %param.10) | copy-start | bytes 5764
  2.5 4.9 %copy-start.1 = (s32[96]{0:T(128)S(1)}, s32[96]{0:T(128)}, u32[]{:S(2)}) copy-start(s32[96]{0:T(128)} %param.11) | copy-start | bytes 1156
  2.5 6.2 %collective-permute-start = (bf16[512,1024]{1,0:T(8,128)(2,1)S(1)}, bf16[512,1024]{1,0:T(8,128)(2,1)}, u32[]{:S(2)}, u32[]{:S(2)}) collective-permute-start(bf16[512,1024]{1,0:T(8,128)(2,1)S(1)} %pad_maximum_fusion), channel_id=1, source_target_pairs={{0,1},{1,0},{2,3},{3,2},{4,5},{5,4},{6,7},{7,6},{8,9},{9,8},{10,11... | collective-permute-start | bytes 3145736 | tf_op jit(solution)/shard_map/ppermute | solution.py:281
  4.3 27.7 %collective-permute-start.1 = (bf16[512,1024]{1,0:T(8,128)(2,1)}, bf16[512,1024]{1,0:T(8,128)(2,1)}, u32[]{:S(2)}, u32[]{:S(2)}) collective-permute-start(bf16[512,1024]{1,0:T(8,128)(2,1)} %pad_maximum_fusion.1), channel_id=1, source_target_pairs={{1,2},{3,4},{5,6},{7,8},{9,10},{11,12},{13,14},{2,1},{4,3},{6,5},{... | collective-permute-start | bytes 3145736 | tf_op jit(solution)/shard_map/ppermute | solution.py:280
  22.7 31.9 %collective-permute-start.2 = (bf16[512,1024]{1,0:T(8,128)(2,1)}, bf16[512,1024]{1,0:T(8,128)(2,1)}, u32[]{:S(2)}, u32[]{:S(2)}) collective-permute-start(bf16[512,1024]{1,0:T(8,128)(2,1)} %get-tuple-element.28), channel_id=1, source_target_pairs={{0,1},{1,0},{2,3},{3,2},{4,5},{5,4},{6,7},{7,6},{8,9},{9,8},{10,11... | collective-permute-start | bytes 3145736 | tf_op jit(solution)/shard_map/ppermute | solution.py:331
  49.0 20.1 %collective-permute-start.4 = (bf16[512,512]{1,0:T(8,128)(2,1)}, bf16[512,512]{1,0:T(8,128)(2,1)}, u32[]{:S(2)}, u32[]{:S(2)}) collective-permute-start(bf16[512,512]{1,0:T(8,128)(2,1)} %get-tuple-element.34), channel_id=1, source_target_pairs={{1,2},{3,4},{5,6},{7,8},{9,10},{11,12},{13,14},{2,1},{4,3},{6,5},{... | collective-permute-start | bytes 1572872 | tf_op jit(solution)/shard_map/ppermute | solution.py:338
  52.0 17.1 %collective-permute-start.3 = (bf16[512,512]{1,0:T(8,128)(2,1)}, bf16[512,512]{1,0:T(8,128)(2,1)}, u32[]{:S(2)}, u32[]{:S(2)}) collective-permute-start(bf16[512,512]{1,0:T(8,128)(2,1)} %get-tuple-element.33), channel_id=1, source_target_pairs={{1,2},{3,4},{5,6},{7,8},{9,10},{11,12},{13,14},{2,1},{4,3},{6,5},{... | collective-permute-start | bytes 1572872 | tf_op jit(solution)/shard_map/ppermute | solution.py:338

commit v2 on v1

--- a/solution.py
+++ b/solution.py
@@ -18,6 +18,7 @@
 DEAD = 1e30
 CHUNKS = 2
 GROUP = 2
+WEIGHTS = 6
 F32 = jnp.float32
 BF16 = jnp.bfloat16
 NT = (((1,), (1,)), ((), ()))
@@ -37,9 +38,10 @@
 
 
 def by_head(x):
-    first_head = lax.broadcasted_iota(jnp.int32, x.shape, 1) < HEAD_DIM
+    x = x.T
+    first_head = lax.broadcasted_iota(jnp.int32, x.shape, 0) < HEAD_DIM
     zero = jnp.zeros_like(x)
-    return jnp.concatenate([jnp.where(first_head, x, zero), jnp.where(first_head, zero, x)], axis=0)
+    return jnp.concatenate([jnp.where(first_head, x, zero), jnp.where(first_head, zero, x)], axis=1)
 
 
 def dead_slots(first, tiles_dev, tile_pairs, counts):
@@ -54,7 +56,7 @@
 
 
 def attend(pairs_here, base, q, do, dq, k_ext, v_ext, kt, dk_acc, dv_acc, dead, bufs):
-    qw, dw, s_buf, dp_buf, p_buf, ds_buf = bufs
+    qw, dw, s_buf, dp_buf, e_buf, ds_buf = bufs
     units = [(g, n) for g in range(pairs_here) for n in range(REACH)]
     half = 32
     state = {}
@@ -66,16 +68,14 @@
 
     def scores(u):
         g, n, lanes, rows, band = at(u)
-        b, w = u % 2, u % 3
+        b, w = u % 2, u % WEIGHTS
 
         def weights():
             qw[w] = by_head(q[rows, lanes])
             dw[w] = by_head(do[rows, lanes])
 
         def product():
-            state[u, "s"] = lax.dot_general(
-                k_ext[band, lanes], qw[w], NT, preferred_element_type=F32
-            )
+            state[u, "s"] = jnp.dot(k_ext[band, lanes], qw[w], preferred_element_type=F32)
 
         def one(o):
             def emit():
@@ -88,15 +88,19 @@
             return emit
 
         def grad_probs():
-            dp_buf[b] = lax.dot_general(v_ext[band, lanes], dw[w], NT, preferred_element_type=F32)
+            dp_buf[b] = jnp.dot(v_ext[band, lanes], dw[w], preferred_element_type=F32)
 
         return [weights, product] + [one(o) for o in range(BAND)] + [grad_probs]
 
     def softmax(u):
-        n, b = units[u][1], u % 2
+        g, n, lanes, rows, band = at(u)
+        b, wide = u % 2, slice(n * 2 * TILE, (n + 1) * 2 * TILE)
 
         def parts(o):
             return [slice(o * TILE + c, o * TILE + c + half) for c in range(0, TILE, half)]
+
+        def shifted(r):
+            return slice(r.start + n * TILE, r.stop + n * TILE)
 
         def fold(x):
             return jnp.sum(x.reshape(half // 8, 8, 2 * TILE), axis=0)
@@ -112,68 +116,87 @@
                 for r in parts(o):
                     e = jnp.exp2(s_buf[b, r] * SCALE_LOG2 - shift)
                     s_buf[b, r] = e
+                    e_buf[g % 2, shifted(r), wide] = e.astype(BF16)
                     state[u, "l"] = state[u, "l"] + fold(e)
+                    state[u, "d"] = state[u, "d"] + fold(e * dp_buf[b, r])
 
             return emit
 
         def total():
-            state[u, "r"] = 1.0 / jnp.sum(state[u, "l"], axis=0, keepdims=True)
-
-        def normal(o):
-            def emit():
-                for r in parts(o):
-                    p = s_buf[b, r] * state[u, "r"]
-                    s_buf[b, r] = p
-                    p_buf[b, r] = p.astype(BF16)
-                    state[u, "d"] = state[u, "d"] + fold(p * dp_buf[b, r])
-
-            return emit
-
-        def delta():
-            state[u, "d"] = jnp.sum(state[u, "d"], axis=0, keepdims=True)
+            r = 1.0 / jnp.sum(state[u, "l"], axis=0, keepdims=True)
+            state[u, "r"] = r
+            state[u, "d"] = jnp.sum(state[u, "d"], axis=0, keepdims=True) * r
 
         def score_grads(o):
             def emit():
                 for r in parts(o):
-                    ds_buf[b, r] = (s_buf[b, r] * (dp_buf[b, r] - state[u, "d"])).astype(BF16)
+                    ds = s_buf[b, r] * (dp_buf[b, r] - state[u, "d"])
+                    ds_buf[g % 2, shifted(r), wide] = ds.astype(BF16)
 
             return emit
 
-        out = [peak] + [powers(o) for o in range(BAND)]
-        out += [total] + [normal(o) for o in range(BAND)]
-        return out + [delta] + [score_grads(o) for o in range(BAND)]
-
-    def grads(u):
+        return (
+            [peak]
+            + [powers(o) for o in range(BAND)]
+            + [total]
+            + [score_grads(o) for o in range(BAND)]
+        )
+
+    def query_grads(u):
         g, n, lanes, rows, band = at(u)
-        b, w = u % 2, u % 3
-
-        def keyed(source, weight, acc):
+        wide = slice(n * 2 * TILE, (n + 1) * 2 * TILE)
+
+        def emit():
+            x = jnp.dot(kt[g, :, band], ds_buf[g % 2, band, wide], preferred_element_type=F32)
+            x = x * (state[u, "r"] * SCALE)
+            first_head = lax.broadcasted_iota(jnp.int32, (PAIR, TILE), 0) < HEAD_DIM
+            dq[rows, lanes] = jnp.where(first_head, x[:, :TILE], x[:, TILE:]).T.astype(BF16)
+
+        return [emit]
+
+    def key_grads(g, source, weight, acc):
+        lanes = slice(g * PAIR, (g + 1) * PAIR)
+        both = slice(0, 4 * TILE)
+
+        def scaled():
+            state[g, "w"] = jnp.concatenate(
+                [
+                    (weight[u % WEIGHTS].astype(F32) * state[u, "r"]).astype(BF16)
+                    for u in (REACH * g, REACH * g + 1)
+                ],
+                axis=1,
+            )
+
+        def rows_of(rows, wide):
             def emit():
-                x = jnp.dot(source[b], weight[w], preferred_element_type=F32)
-                if n == 0:
-                    acc[band, lanes] = x
-                else:
-                    shared = slice(n * TILE, BAND * TILE)
-                    acc[shared, lanes] = acc[shared, lanes] + x[: (BAND - n) * TILE]
-                    acc[BAND * TILE :, lanes] = x[(BAND - n) * TILE :]
+                acc[rows, lanes] = lax.dot_general(
+                    source[g % 2, rows, wide],
+                    state[g, "w"][:, wide],
+                    NT,
+                    preferred_element_type=F32,
+                )
 
             return emit
 
-        def query():
-            x = jnp.dot(kt[g, :, band], ds_buf[b], preferred_element_type=F32)
-            first_head = lax.broadcasted_iota(jnp.int32, (PAIR, TILE), 0) < HEAD_DIM
-            dq[rows, lanes] = (
-                jnp.where(first_head, x[:, :TILE], x[:, TILE:]).T * SCALE
-            ).astype(BF16)
-
-        return [keyed(p_buf, dw, dv_acc), query, keyed(ds_buf, qw, dk_acc)]
+        return [
+            scaled,
+            rows_of(slice(0, TILE), slice(0, 2 * TILE)),
+            rows_of(slice(TILE, BAND * TILE), both),
+            rows_of(slice(BAND * TILE, KEYS), slice(2 * TILE, 4 * TILE)),
+        ]
 
     count = len(units)
-    for step in range(count + 2):
+    for step in range(count + 3):
+        late = []
+        if 0 <= step - 2 < count:
+            late += query_grads(step - 2)
+        g, odd = divmod(step - 3, 2)
+        if 0 <= g < pairs_here:
+            late += key_grads(g, *((ds_buf, qw, dk_acc) if odd else (e_buf, dw, dv_acc)))
         merge(
             scores(step) if step < count else [],
             softmax(step - 1) if 0 <= step - 1 < count else [],
-            grads(step - 2) if 0 <= step - 2 < count else [],
+            late,
         )
 
 
@@ -185,12 +208,12 @@
         pltpu.VMEM((group, PAIR, KEYS), BF16),
         pltpu.VMEM((KEYS, lanes), F32),
         pltpu.VMEM((KEYS, lanes), F32),
-        pltpu.VMEM((3, 2 * TILE, PAIR), BF16),
-        pltpu.VMEM((3, 2 * TILE, PAIR), BF16),
+        pltpu.VMEM((WEIGHTS, PAIR, 2 * TILE), BF16),
+        pltpu.VMEM((WEIGHTS, PAIR, 2 * TILE), BF16),
         pltpu.VMEM((2, band, 2 * TILE), F32),
         pltpu.VMEM((2, band, 2 * TILE), F32),
-        pltpu.VMEM((2, band, 2 * TILE), BF16),
-        pltpu.VMEM((2, band, 2 * TILE), BF16),
+        pltpu.VMEM((2, KEYS, 4 * TILE), BF16),
+        pltpu.VMEM((2, KEYS, 4 * TILE), BF16),
     ]
 
 

time: 72.5 us -> 70.4 us (0.971)
  Pallas kernels: 48.3 us -> 45.2 us
  waiting for transfers between devices: 8.79 us -> 9.84 us
    pallas_call x3, Pallas kernels: 31 us -> 29 us  [edge(): pl.pallas_call(functools.partial(edge_kernel, group, len(aliases)), grid_...]
    ppermute x1, waiting for transfers between devices: 8.78 us -> 9.83 us  [shards(): cross_halo = lax.ppermute(cross_out, 'seq', cross_swap)]
    pallas_call x1, Pallas kernels: 14.5 us -> 13.5 us  [shards(): pl.pallas_call(functools.partial(inner_kernel, GROUP), grid_spec=pltpu.Pr...]
  transfers between devices with their start and end apart: 5 -> 5, of which waited for: 1 -> 1; matrix products, arithmetic and copies ran while one was open for 3% -> 3% of each run, Pallas kernels for 63% -> 61%
where the time goes in v2:
time: 70.4 us; the launch traced here: 69.8 us
  Pallas kernels  45.2 us (64%)
  waiting for transfers between devices  9.84 us (14%)
  starting transfers between devices  9.74 us (14%)
  other arithmetic  2.12 us (3%)
  local copies, waits for them, and re-layouts  2.1 us (3%)
  between operations  0.74 us (1%)
    pallas_call x3, Pallas kernels, edge(): pl.pallas_call(functools.partial(edge_kernel, group, len(aliases)), grid_...  29 us
    pallas_call x1, Pallas kernels, shards(): pl.pallas_call(functools.partial(inner_kernel, GROUP), grid_spec=pltpu.Pr...  13.5 us
    ppermute x1, waiting for transfers between devices, shards(): cross_halo = lax.ppermute(cross_out, 'seq', cross_swap)  9.83 us
    ppermute x2, starting transfers between devices, shards(): cross_back.append(lax.ppermute(send, 'seq', cross_swap))  5.55 us
    ppermute x1, starting transfers between devices, shards(): cross_halo = lax.ppermute(cross_out, 'seq', cross_swap)  3.04 us
    pallas_call x1, Pallas kernels, shards(): pl.pallas_call(join_kernel, grid_spec=pltpu.PrefetchScalarGridSpec(num_sc...  2.67 us
    dynamic_slice x1, local copies, waits for them, and re-layouts, pack(): lax.dynamic_slice_in_dim(x[:, columns], block * BLOCK, BLOCK, 0)  1.74 us
  transfers between devices with their start and end apart: 5, of which 1 were waited for; matrix products, arithmetic and copies ran while one was open for 3% of the time, Pallas kernels for 61%

profile of v2, /device:TPU:17, one launch (start us, length us, event | category | flops | bytes accessed | tf_op | source)
XLA Modules:
  0.0 69.8 jit_solution(16405828035684502188)
XLA Ops:
  0.6 0.0 copy-start
  0.7 1.7 %constant_dynamic-slice_fusion = (bf16[256,1024]{1,0:T(8,128)(2,1)S(1)}, bf16[256,1024]{1,0:T(8,128)(2,1)S(1)}, bf16[256,1024]{1,0:T(8,128)(2,1)S(1)}, bf16[256,1024]{1,0:T(8,128)(2,1)S(1)}) fusion(bf16[768,1024]{1,0:T(8,128)(2,1)} %v.1, s32[]{:T(128)S(6)} %select_n.32, s32[]{:T(128)S(6)} %select_n.31, bf16[768,1024]{1,0:T(8,128)(2,1)} %k.1), kind=kLoop, calls=%fused_computation.6 | loop fusion | bytes 4194312 | tf_op jit(solution)/shard_map/dynamic_slice | solution.py:295
  2.4 0.1 pad_maximum_fusion
  2.5 0.0 copy-start.1
  2.5 0.7 %collective-permute-start = (bf16[512,1024]{1,0:T(8,128)(2,1)S(1)}, bf16[512,1024]{1,0:T(8,128)(2,1)}, u32[]{:S(2)}, u32[]{:S(2)}) collective-permute-start(bf16[512,1024]{1,0:T(8,128)(2,1)S(1)} %pad_maximum_fusion), channel_id=1, source_target_pairs={{0,1},{1,0},{2,3},{3,2},{4,5},{5,4},{6,7},{7,6},{8,9},{9,8},{10,11... | collective-permute-start | bytes 3145736 | tf_op jit(solution)/shard_map/ppermute | solution.py:304
  3.2 1.0 %pad_maximum_fusion.1 = bf16[512,1024]{1,0:T(8,128)(2,1)} fusion(bf16[256,1024]{1,0:T(8,128)(2,1)S(1)} %get-tuple-element.39, bf16[256,1024]{1,0:T(8,128)(2,1)S(1)} %get-tuple-element.42), kind=kLoop, calls=%fused_computation.1 | loop fusion | flops 2097152 | bytes 2097152 | tf_op jit(solution)/shard_map/concatenate | solution.py:293
  4.3 3.0 %collective-permute-start.1 = (bf16[512,1024]{1,0:T(8,128)(2,1)}, bf16[512,1024]{1,0:T(8,128)(2,1)}, u32[]{:S(2)}, u32[]{:S(2)}) collective-permute-start(bf16[512,1024]{1,0:T(8,128)(2,1)} %pad_maximum_fusion.1), channel_id=1, source_target_pairs={{1,2},{3,4},{5,6},{7,8},{9,10},{11,12},{13,14},{2,1},{4,3},{6,5},{... | collective-permute-start | bytes 3145736 | tf_op jit(solution)/shard_map/ppermute | solution.py:303
  7.3 0.1 constant_dynamic-slice_fusion.4
  7.4 0.1 dynamic_slice.19
  7.5 0.1 copy.17
  7.6 0.1 broadcast_add_fusion
  7.7 0.1 iota_compare_fusion
  7.7 0.3 and_reduce_fusion
  8.0 0.1 copy.18
  8.1 0.6 broadcast_select_fusion.dead
  8.7 13.0 %edge_tiles.3 = (bf16[768,1024]{1,0:T(8,128)(2,1)}, f32[512,1024]{1,0:T(8,128)}, f32[512,1024]{1,0:T(8,128)}, bf16[512,1024]{1,0:T(8,128)(2,1)}) custom-call(s32[1]{0:T(128)} %bitcast.1.place, f32[6,5]{1,0:T(8,128)} %broadcast_select_fusion.dead, bf16[768,1024]{1,0:T(8,128)(2,1)} %q.7, bf16[768,1024]{1,0:T(8,128)(2,1)} %do.7, bf16[768,1024]{1,0:T(8,128)(2,1)} %k.1, ...), custom_call_target="tpu_custom_call" | custom-call | flops 1 | bytes 1 | tf_op jit(solution)/shard_map/edge_tiles/pallas_call | solution.py:331
  21.7 0.4 collective-permute-start.2
  22.1 9.8 %collective-permute-done.1.halo = bf16[512,1024]{1,0:T(8,128)(2,1)} collective-permute-done((bf16[512,1024]{1,0:T(8,128)(2,1)}, bf16[512,1024]{1,0:T(8,128)(2,1)}, u32[]{:S(2)}, u32[]{:S(2)}) %collective-permute-start.1) | collective-permute-done | bytes 1048608 | tf_op jit(solution)/shard_map/ppermute | solution.py:303
  31.9 8.0 %edge_tiles.4 = (bf16[768,1024]{1,0:T(8,128)(2,1)}, f32[512,1024]{1,0:T(8,128)}, f32[512,1024]{1,0:T(8,128)}, bf16[512,512]{1,0:T(8,128)(2,1)}) custom-call(s32[1]{0:T(128)} %bitcast.place, f32[6,5]{1,0:T(8,128)} %broadcast_select_fusion.dead, bf16[768,1024]{1,0:T(8,128)(2,1)} %q.7, bf16[768,1024]{1,0:T(8,128)(2,1)} %do.7, ...), custom_call_target="tpu_custom_call", output_to_operand_aliasing={{0}: (9, {})} | custom-call | flops 1 | bytes 1 | tf_op jit(solution)/shard_map/edge_tiles/pallas_call | solution.py:331
  39.9 8.0 %edge_tiles.5 = (bf16[768,1024]{1,0:T(8,128)(2,1)}, f32[512,1024]{1,0:T(8,128)}, f32[512,1024]{1,0:T(8,128)}, bf16[512,512]{1,0:T(8,128)(2,1)}) custom-call(s32[1]{0:T(128)} %bitcast.place, f32[6,5]{1,0:T(8,128)} %broadcast_select_fusion.dead, bf16[768,1024]{1,0:T(8,128)(2,1)} %q.7, ...), custom_call_target="tpu_custom_call", output_to_operand_aliasing={{0}: (9, {}), {1}: (10, {}), {2}: (11, {})} | custom-call | flops 1 | bytes 1 | tf_op jit(solution)/shard_map/edge_tiles/pallas_call | solution.py:331
  48.0 3.0 %collective-permute-start.4 = (bf16[512,512]{1,0:T(8,128)(2,1)}, bf16[512,512]{1,0:T(8,128)(2,1)}, u32[]{:S(2)}, u32[]{:S(2)}) collective-permute-start(bf16[512,512]{1,0:T(8,128)(2,1)} %get-tuple-element.34), channel_id=1, source_target_pairs={{1,2},{3,4},{5,6},{7,8},{9,10},{11,12},{13,14},{2,1},{4,3},{6,5},{... | collective-permute-start | bytes 1572872 | tf_op jit(solution)/shard_map/ppermute | solution.py:361
  51.0 2.5 %collective-permute-start.3 = (bf16[512,512]{1,0:T(8,128)(2,1)}, bf16[512,512]{1,0:T(8,128)(2,1)}, u32[]{:S(2)}, u32[]{:S(2)}) collective-permute-start(bf16[512,512]{1,0:T(8,128)(2,1)} %get-tuple-element.33), channel_id=1, source_target_pairs={{1,2},{3,4},{5,6},{7,8},{9,10},{11,12},{13,14},{2,1},{4,3},{6,5},{... | collective-permute-start | bytes 1572872 | tf_op jit(solution)/shard_map/ppermute | solution.py:361
  53.6 13.5 %inner_tiles.1 = (bf16[768,1024]{1,0:T(8,128)(2,1)}, bf16[768,1024]{1,0:T(8,128)(2,1)}, bf16[768,1024]{1,0:T(8,128)(2,1)}) custom-call(s32[1]{0:T(128)} %bitcast.place, f32[6,5]{1,0:T(8,128)} %broadcast_select_fusion.dead, bf16[768,1024]{1,0:T(8,128)(2,1)} %q.7, bf16[768,1024]{1,0:T(8,128)(2,1)} %do.7, ...), custom_call_target="tpu_custom_call", output_to_operand_aliasing={{0}: (11, {})} | custom-call | flops 1 | bytes 1 | tf_op jit(solution)/shard_map/inner_tiles/pallas_call | solution.py:370
  67.1 2.7 %join_edges.1 = (bf16[768,1024]{1,0:T(8,128)(2,1)}, bf16[768,1024]{1,0:T(8,128)(2,1)}) custom-call(s32[1]{0:T(128)} %bitcast.place, bf16[768,1024]{1,0:T(8,128)(2,1)} %get-tuple-element.31.dk, bf16[768,1024]{1,0:T(8,128)(2,1)} %get-tuple-element.32.dv, ...), custom_call_target="tpu_custom_call", output_to_operand_aliasing={{0}: (1, {}), {1}: (2, {})} | custom-call | flops 1 | bytes 1 | tf_op jit(solution)/shard_map/join_edges/pallas_call | solution.py:390
  (8 shorter events, 0.0 us)
Async XLA Ops:
  0.6 6.7 %copy-start = (s32[96,5]{0,1:T(8,128)S(1)}, s32[96,5]{0,1:T(8,128)}, u32[]{:S(2)}) copy-start(s32[96,5]{0,1:T(8,128)} %param.10) | copy-start | bytes 5764
  2.5 4.9 %copy-start.1 = (s32[96]{0:T(128)S(1)}, s32[96]{0:T(128)}, u32[]{:S(2)}) copy-start(s32[96]{0:T(128)} %param.11) | copy-start | bytes 1156
  2.5 6.2 %collective-permute-start = (bf16[512,1024]{1,0:T(8,128)(2,1)S(1)}, bf16[512,1024]{1,0:T(8,128)(2,1)}, u32[]{:S(2)}, u32[]{:S(2)}) collective-permute-start(bf16[512,1024]{1,0:T(8,128)(2,1)S(1)} %pad_maximum_fusion), channel_id=1, source_target_pairs={{0,1},{1,0},{2,3},{3,2},{4,5},{5,4},{6,7},{7,6},{8,9},{9,8},{10,11... | collective-permute-start | bytes 3145736 | tf_op jit(solution)/shard_map/ppermute | solution.py:304
  4.3 27.7 %collective-permute-start.1 = (bf16[512,1024]{1,0:T(8,128)(2,1)}, bf16[512,1024]{1,0:T(8,128)(2,1)}, u32[]{:S(2)}, u32[]{:S(2)}) collective-permute-start(bf16[512,1024]{1,0:T(8,128)(2,1)} %pad_maximum_fusion.1), channel_id=1, source_target_pairs={{1,2},{3,4},{5,6},{7,8},{9,10},{11,12},{13,14},{2,1},{4,3},{6,5},{... | collective-permute-start | bytes 3145736 | tf_op jit(solution)/shard_map/ppermute | solution.py:303
  21.7 31.9 %collective-permute-start.2 = (bf16[512,1024]{1,0:T(8,128)(2,1)}, bf16[512,1024]{1,0:T(8,128)(2,1)}, u32[]{:S(2)}, u32[]{:S(2)}) collective-permute-start(bf16[512,1024]{1,0:T(8,128)(2,1)} %get-tuple-element.28), channel_id=1, source_target_pairs={{0,1},{1,0},{2,3},{3,2},{4,5},{5,4},{6,7},{7,6},{8,9},{9,8},{10,11... | collective-permute-start | bytes 3145736 | tf_op jit(solution)/shard_map/ppermute | solution.py:354
  48.0 19.1 %collective-permute-start.4 = (bf16[512,512]{1,0:T(8,128)(2,1)}, bf16[512,512]{1,0:T(8,128)(2,1)}, u32[]{:S(2)}, u32[]{:S(2)}) collective-permute-start(bf16[512,512]{1,0:T(8,128)(2,1)} %get-tuple-element.34), channel_id=1, source_target_pairs={{1,2},{3,4},{5,6},{7,8},{9,10},{11,12},{13,14},{2,1},{4,3},{6,5},{... | collective-permute-start | bytes 1572872 | tf_op jit(solution)/shard_map/ppermute | solution.py:361
  51.0 16.1 %collective-permute-start.3 = (bf16[512,512]{1,0:T(8,128)(2,1)}, bf16[512,512]{1,0:T(8,128)(2,1)}, u32[]{:S(2)}, u32[]{:S(2)}) collective-permute-start(bf16[512,512]{1,0:T(8,128)(2,1)} %get-tuple-element.33), channel_id=1, source_target_pairs={{1,2},{3,4},{5,6},{7,8},{9,10},{11,12},{13,14},{2,1},{4,3},{6,5},{... | collective-permute-start | bytes 1572872 | tf_op jit(solution)/shard_map/ppermute | solution.py:361

commit v3 on v2

--- a/solution.py
+++ b/solution.py
@@ -16,7 +16,7 @@
 BLOCK = REACH * TILE
 PAIR = 2 * HEAD_DIM
 DEAD = 1e30
-CHUNKS = 2
+CUTS = (0, 4, 8)
 GROUP = 2
 WEIGHTS = 6
 F32 = jnp.float32
@@ -55,7 +55,7 @@
     return jnp.where(hit, 0.0, DEAD).astype(F32)
 
 
-def attend(pairs_here, base, q, do, dq, k_ext, v_ext, kt, dk_acc, dv_acc, dead, bufs):
+def attend(pairs_here, base, q, do, dq, k_ext, v_ext, kt, dk_acc, dv_acc, dead, bufs, finish):
     qw, dw, s_buf, dp_buf, e_buf, ds_buf = bufs
     units = [(g, n) for g in range(pairs_here) for n in range(REACH)]
     half = 32
@@ -185,9 +185,27 @@
             rows_of(slice(BAND * TILE, KEYS), slice(2 * TILE, 4 * TILE)),
         ]
 
+    def transposed(g):
+        lanes = slice(g * PAIR, (g + 1) * PAIR)
+
+        def one(j):
+            def emit():
+                rows = slice(j * TILE, (j + 1) * TILE)
+                kt[g, :, rows] = k_ext[rows, lanes].T
+
+            return emit
+
+        return [one(j) for j in range(KEY_TILES)]
+
     count = len(units)
-    for step in range(count + 3):
+    for step in range(count + 4):
         late = []
+        g, odd = divmod(step - 4, 2)
+        if 0 <= g < pairs_here:
+            late.append(functools.partial(finish, odd == 1, slice(g * PAIR, (g + 1) * PAIR)))
+        g, odd = divmod(step - 1, 2)
+        if 0 <= g < pairs_here and odd == 0:
+            late += transposed(g)
         if 0 <= step - 2 < count:
             late += query_grads(step - 2)
         g, odd = divmod(step - 3, 2)
@@ -217,13 +235,6 @@
     ]
 
 
-def transpose_keys(group, k_ext, kt):
-    for g in range(group):
-        for j in range(KEY_TILES):
-            rows = slice(j * TILE, (j + 1) * TILE)
-            kt[g, :, rows] = k_ext[rows, g * PAIR : (g + 1) * PAIR].T
-
-
 def edge_kernel(group, chained, place, dead, q, do, k_near, k_mid, v_near, v_mid, halo, *rest):
     rest = rest[chained:]
     dq, part_k, part_v, send, k_ext, v_ext, kt, dk_acc, dv_acc, *bufs = rest
@@ -235,12 +246,17 @@
         ext[pl.ds(outside, BLOCK)] = halo[row : row + BLOCK]
         ext[BLOCK : 2 * BLOCK] = near[...]
         ext[pl.ds(inside, BLOCK)] = mid[...]
-    transpose_keys(group, k_ext, kt)
-    attend(group, place[0] * REACH, q, do, dq, k_ext, v_ext, kt, dk_acc, dv_acc, dead, bufs)
-    for acc, part, row, scale in ((dk_acc, part_k, 0, SCALE), (dv_acc, part_v, BLOCK, 1.0)):
-        send[row : row + BLOCK] = (acc[pl.ds(outside, BLOCK)] * scale).astype(BF16)
-        part[:BLOCK] = acc[BLOCK : 2 * BLOCK]
-        part[BLOCK:] = acc[pl.ds(inside, BLOCK)]
+
+    def finish(keys, lanes):
+        acc, part, row, scale = (
+            (dk_acc, part_k, 0, SCALE) if keys else (dv_acc, part_v, BLOCK, 1.0)
+        )
+        send[row : row + BLOCK, lanes] = (acc[pl.ds(outside, BLOCK), lanes] * scale).astype(BF16)
+        part[:BLOCK, lanes] = acc[BLOCK : 2 * BLOCK, lanes].astype(BF16)
+        part[BLOCK:, lanes] = acc[pl.ds(inside, BLOCK), lanes].astype(BF16)
+
+    base = place[0] * REACH
+    attend(group, base, q, do, dq, k_ext, v_ext, kt, dk_acc, dv_acc, dead, bufs, finish)
 
 
 def inner_kernel(
@@ -250,26 +266,38 @@
     cross = pl.multiple_of(place[0] * BLOCK, BLOCK)
     chip = pl.multiple_of(2 * BLOCK - cross, BLOCK)
 
-    transpose_keys(group, k, kt)
-    attend(group, REACH, q, do, dq, k, v, kt, dk_acc, dv_acc, dead, bufs)
-    for acc, part, other, row, out, scale in (
-        (dk_acc, chip_k, cross_k, 0, dk, SCALE),
-        (dv_acc, chip_v, cross_v, BLOCK, dv, 1.0),
-    ):
-        out[pl.ds(cross, BLOCK)] = ((acc[pl.ds(cross, BLOCK)] + other[:BLOCK]) * scale).astype(BF16)
-        middle = acc[BLOCK : 2 * BLOCK] + part[BLOCK:] + other[BLOCK:]
-        out[BLOCK : 2 * BLOCK] = (middle * scale).astype(BF16)
-        edge = (acc[pl.ds(chip, BLOCK)] + part[:BLOCK]) * scale
-        out[pl.ds(chip, BLOCK)] = (edge + back[row : row + BLOCK].astype(F32)).astype(BF16)
-
-
-def join_kernel(place, dk, dv, *rest):
-    *backs, dk_out, dv_out = rest
-    span = backs[0].shape[1]
-    for c, back in enumerate(backs):
-        lanes = slice(c * span, (c + 1) * span)
-        dk_out[:, lanes] = (dk[:, lanes].astype(F32) + back[:BLOCK].astype(F32)).astype(BF16)
-        dv_out[:, lanes] = (dv[:, lanes].astype(F32) + back[BLOCK:].astype(F32)).astype(BF16)
+
+    def finish(keys, lanes):
+        acc, part, other, row, out, scale = (
+            (dk_acc, chip_k, cross_k, 0, dk, SCALE)
+            if keys
+            else (dv_acc, chip_v, cross_v, BLOCK, dv, 1.0)
+        )
+        near = acc[pl.ds(cross, BLOCK), lanes] + other[:BLOCK, lanes].astype(F32)
+        out[pl.ds(cross, BLOCK), lanes] = (near * scale).astype(BF16)
+        middle = acc[BLOCK : 2 * BLOCK, lanes] + part[BLOCK:, lanes].astype(F32)
+        middle = middle + other[BLOCK:, lanes].astype(F32)
+        out[BLOCK : 2 * BLOCK, lanes] = (middle * scale).astype(BF16)
+        far = (acc[pl.ds(chip, BLOCK), lanes] + part[:BLOCK, lanes].astype(F32)) * scale
+        far = far + back[row : row + BLOCK, lanes].astype(F32)
+        out[pl.ds(chip, BLOCK), lanes] = far.astype(BF16)
+
+    attend(group, REACH, q, do, dq, k, v, kt, dk_acc, dv_acc, dead, bufs, finish)
+
+
+def pack_kernel(place, k_cross, k_chip, v_cross, v_chip, *outs):
+    *cross_out, chip_out = outs
+    for row, cross, chip in ((0, k_cross, k_chip), (BLOCK, v_cross, v_chip)):
+        chip_out[row : row + BLOCK] = chip[...]
+        at = 0
+        for out in cross_out:
+            out[row : row + BLOCK] = cross[:, at : at + out.shape[1]]
+            at += out.shape[1]
+
+
+def join_kernel(place, dk, dv, back, dk_out, dv_out):
+    dk_out[...] = (dk[...].astype(F32) + back[:BLOCK].astype(F32)).astype(BF16)
+    dv_out[...] = (dv[...].astype(F32) + back[BLOCK:].astype(F32)).astype(BF16)
 
 
 def shards(queries, key_states, values, grad_out, tile_pairs, counts):
@@ -285,23 +313,31 @@
     cross_place = jnp.reshape(cross_block, (1,)).astype(jnp.int32)
     chip_place = jnp.reshape(2 - cross_block, (1,)).astype(jnp.int32)
     dead = dead_slots(first, tiles_dev, tile_pairs, counts)
-    span = width // CHUNKS
     params = pltpu.CompilerParams(vmem_limit_bytes=VMEM_BYTES)
     cost = pl.CostEstimate(flops=1, bytes_accessed=1, transcendentals=0)
 
-    def pack(block, columns):
-        return jnp.concatenate(
-            [
-                lax.dynamic_slice_in_dim(x[:, columns], block * BLOCK, BLOCK, 0)
-                for x in (key_states, values)
-            ],
-            axis=0,
-        )
-
-    chunks = [slice(c * span, (c + 1) * span) for c in range(CHUNKS)]
-    cross_out = pack(cross_block, slice(0, width))
-    cross_halo = lax.ppermute(cross_out, "seq", cross_swap)
-    chip_halo = lax.ppermute(pack(2 - cross_block, slice(0, width)), "seq", chip_swap)
+    eighth = width // CUTS[-1]
+    chunks = [slice(a * eighth, b * eighth) for a, b in zip(CUTS, CUTS[1:])]
+    spans = [c.stop - c.start for c in chunks]
+    cross_edge = pl.BlockSpec((BLOCK, width), lambda h, place: (place[0], 0))
+    chip_edge = pl.BlockSpec((BLOCK, width), lambda h, place: (2 - place[0], 0))
+    *cross_out, chip_out = pl.pallas_call(
+        pack_kernel,
+        grid_spec=pltpu.PrefetchScalarGridSpec(
+            num_scalar_prefetch=1,
+            grid=(1,),
+            in_specs=[cross_edge, chip_edge] * 2,
+            out_specs=[pl.BlockSpec((2 * BLOCK, span), lambda h, *_: (0, 0)) for span in spans]
+            + [pl.BlockSpec((2 * BLOCK, width), lambda h, *_: (0, 0))],
+        ),
+        out_shape=[jax.ShapeDtypeStruct((2 * BLOCK, span), BF16) for span in spans]
+        + [jax.ShapeDtypeStruct((2 * BLOCK, width), BF16)],
+        compiler_params=params,
+        cost_estimate=cost,
+        name="pack_edges",
+    )(cross_place, key_states, key_states, values, values)
+    cross_halos = [lax.ppermute(x, "seq", cross_swap) for x in cross_out]
+    chip_halo = lax.ppermute(chip_out, "seq", chip_swap)
 
     def edge(place, halo, column, lanes, earlier):
         group = min(GROUP, lanes // PAIR)
@@ -320,7 +356,7 @@
         one = pl.BlockSpec((BLOCK, wide), near)
         two = pl.BlockSpec((BLOCK, wide), mid)
         double = pl.BlockSpec((2 * BLOCK, wide), own)
-        halo_block = pl.BlockSpec((2 * BLOCK, wide), lambda h, *_: (0, at + h))
+        wide_double = pl.BlockSpec((2 * BLOCK, wide), lambda h, *_: (0, at + h))
         operands = [place, dead, queries, grad_out, key_states, key_states]
         operands += [values, values, halo]
         aliases = {}
@@ -333,15 +369,15 @@
             grid_spec=pltpu.PrefetchScalarGridSpec(
                 num_scalar_prefetch=2,
                 grid=(lanes // wide,),
-                in_specs=[one, one, one, two, one, two, halo_block]
+                in_specs=[one, one, one, two, one, two, double]
                 + [pl.BlockSpec(memory_space=pl.ANY)] * len(aliases),
-                out_specs=[one, halo_block, halo_block, double],
+                out_specs=[one, wide_double, wide_double, double],
                 scratch_shapes=scratch(group),
             ),
             out_shape=[
                 jax.ShapeDtypeStruct((rows_dev, width), BF16),
-                jax.ShapeDtypeStruct((2 * BLOCK, width), F32),
-                jax.ShapeDtypeStruct((2 * BLOCK, width), F32),
+                jax.ShapeDtypeStruct((2 * BLOCK, width), BF16),
+                jax.ShapeDtypeStruct((2 * BLOCK, width), BF16),
                 jax.ShapeDtypeStruct((2 * BLOCK, lanes), BF16),
             ],
             input_output_aliases=aliases,
@@ -354,9 +390,9 @@
     chip_back = lax.ppermute(chip_send, "seq", chip_swap)
     cross_k = cross_v = None
     cross_back = []
-    for c in chunks:
+    for c, halo in zip(chunks, cross_halos):
         dq, cross_k, cross_v, send = edge(
-            cross_place, cross_halo, c.start, span, [dq, cross_k, cross_v]
+            cross_place, halo, c.start, c.stop - c.start, [dq, cross_k, cross_v]
         )
         cross_back.append(lax.ppermute(send, "seq", cross_swap))
 
@@ -386,22 +422,24 @@
         name="inner_tiles",
     )(*operands)
 
-    edge_spec = pl.BlockSpec((BLOCK, width), lambda h, place: (place[0], 0))
-    grad_keys, grad_values = pl.pallas_call(
-        join_kernel,
-        grid_spec=pltpu.PrefetchScalarGridSpec(
-            num_scalar_prefetch=1,
-            grid=(1,),
-            in_specs=[edge_spec] * 2
-            + [pl.BlockSpec((2 * BLOCK, span), lambda h, *_: (0, 0))] * CHUNKS,
-            out_specs=[edge_spec] * 2,
-        ),
-        out_shape=[jax.ShapeDtypeStruct((rows_dev, width), BF16)] * 2,
-        input_output_aliases={1: 0, 2: 1},
-        compiler_params=params,
-        cost_estimate=cost,
-        name="join_edges",
-    )(cross_place, grad_keys, grad_values, *cross_back)
+    for c, span, back in zip(chunks, spans, cross_back):
+        at = c.start // span
+        edge_spec = pl.BlockSpec((BLOCK, span), lambda h, place, at=at: (place[0], at))
+        back_spec = pl.BlockSpec((2 * BLOCK, span), lambda h, *_: (0, 0))
+        grad_keys, grad_values = pl.pallas_call(
+            join_kernel,
+            grid_spec=pltpu.PrefetchScalarGridSpec(
+                num_scalar_prefetch=1,
+                grid=(1,),
+                in_specs=[edge_spec, edge_spec, back_spec],
+                out_specs=[edge_spec, edge_spec],
+            ),
+            out_shape=[jax.ShapeDtypeStruct((rows_dev, width), BF16)] * 2,
+            input_output_aliases={1: 0, 2: 1},
+            compiler_params=params,
+            cost_estimate=cost,
+            name="join_edges",
+        )(cross_place, grad_keys, grad_values, back)
     return (dq, grad_keys, grad_values)
 
 

time: 70.4 us -> 69 us (0.980)
  waiting for transfers between devices: 9.84 us -> 4.64 us
  starting transfers between devices: 9.74 us -> 12.9 us
  Pallas kernels: 45.2 us -> 48.1 us
  local copies, waits for them, and re-layouts: 2.1 us -> 0.36 us
  other arithmetic: 2.12 us -> 1.01 us
    ppermute x2 -> x3, waiting for transfers between devices: 9.83 us -> 4.63 us  [the longest x2 3.03 us: shards(): cross_halos = [lax.ppermute(x, 'seq', cross_swap) for x in cross_out]]
    ppermute x2 -> x3, starting transfers between devices: 3.78 us -> 7.17 us  [the longest x2 7.09 us: shards(): cross_halos = [lax.ppermute(x, 'seq', cross_swap) for x in cross_out]]
    pallas_call x0 -> x1, Pallas kernels: none -> 2.87 us  [shards(): pl.pallas_call(pack_kernel, grid_spec=pltpu.PrefetchScalarGridSpec(num_sc...]
    dynamic_slice x1 -> x0, local copies, waits for them, and re-layouts: 1.74 us -> none  [pack(): lax.dynamic_slice_in_dim(x[:, columns], block * BLOCK, BLOCK, 0)]
    pallas_call x1 -> x2, Pallas kernels: 2.67 us -> 4.11 us  [shards(): pl.pallas_call(join_kernel, grid_spec=pltpu.PrefetchScalarGridSpec(num_sc...]
    concatenate x2 -> x0, other arithmetic: 1.11 us -> none  [pack(): jnp.concatenate([lax.dynamic_slice_in_dim(x[:, columns], block * BLOCK, B...]
    pallas_call x1, Pallas kernels: 13.5 us -> 12.8 us  [shards(): pl.pallas_call(functools.partial(inner_kernel, GROUP), grid_spec=pltpu.Pr...]
  transfers between devices with their start and end apart: 5 -> 6, of which waited for: 1 -> 2; matrix products, arithmetic and copies ran while one was open for 3% -> 2% of each run, Pallas kernels for 61% -> 64%
where the time goes in v3:
time: 69 us; the launch traced here: 67.7 us
  Pallas kernels  48.1 us (70%)
  starting transfers between devices  12.9 us (19%)
  waiting for transfers between devices  4.64 us (7%)
  other arithmetic  1.01 us (1%)
  between operations  0.74 us (1%)
    pallas_call x3, Pallas kernels, edge(): pl.pallas_call(functools.partial(edge_kernel, group, len(aliases)), grid_...  28.3 us
    pallas_call x1, Pallas kernels, shards(): pl.pallas_call(functools.partial(inner_kernel, GROUP), grid_spec=pltpu.Pr...  12.8 us
    ppermute x2, starting transfers between devices, shards(): cross_halos = [lax.ppermute(x, 'seq', cross_swap) for x in cross_out]  7.09 us
    ppermute x2, starting transfers between devices, shards(): cross_back.append(lax.ppermute(send, 'seq', cross_swap))  5.54 us
    pallas_call x2, Pallas kernels, shards(): pl.pallas_call(join_kernel, grid_spec=pltpu.PrefetchScalarGridSpec(num_sc...  4.11 us
    ppermute x2, waiting for transfers between devices, shards(): cross_halos = [lax.ppermute(x, 'seq', cross_swap) for x in cross_out]  3.03 us
    pallas_call x1, Pallas kernels, shards(): pl.pallas_call(pack_kernel, grid_spec=pltpu.PrefetchScalarGridSpec(num_sc...  2.87 us
    ppermute x1, waiting for transfers between devices, shards(): chip_halo = lax.ppermute(chip_out, 'seq', chip_swap)  1.61 us
  transfers between devices with their start and end apart: 6, of which 2 were waited for; matrix products, arithmetic and copies ran while one was open for 2% of the time, Pallas kernels for 64%

profile of v3, /device:TPU:17, one launch (start us, length us, event | category | flops | bytes accessed | tf_op | source)
XLA Modules:
  0.0 67.7 jit_solution(477378277846647094)
XLA Ops:
  0.6 0.0 copy-start
  0.7 2.9 %pack_edges.1 = (bf16[512,512]{1,0:T(8,128)(2,1)}, bf16[512,512]{1,0:T(8,128)(2,1)}, bf16[512,1024]{1,0:T(8,128)(2,1)}) custom-call(s32[1]{0:T(128)} %bitcast.place, bf16[768,1024]{1,0:T(8,128)(2,1)} %k.1, bf16[768,1024]{1,0:T(8,128)(2,1)} %k.1, bf16[768,1024]{1,0:T(8,128)(2,1)} %v.1, bf16[768,1024]{1,0:T(8,128)(2,1)} %v.1), custom_call_target="tpu_custom_call" | custom-call | flops 1 | bytes 1 | tf_op jit(solution)/shard_map/pack_edges/pallas_call | solution.py:324
  3.5 3.7 %collective-permute-start.2 = (bf16[512,512]{1,0:T(8,128)(2,1)}, bf16[512,512]{1,0:T(8,128)(2,1)}, u32[]{:S(2)}, u32[]{:S(2)}) collective-permute-start(bf16[512,512]{1,0:T(8,128)(2,1)} %get-tuple-element.29), channel_id=1, source_target_pairs={{1,2},{3,4},{5,6},{7,8},{9,10},{11,12},{13,14},{2,1},{4,3},{6,5},{... | collective-permute-start | bytes 1572872 | tf_op jit(solution)/shard_map/ppermute | solution.py:339
  7.2 0.1 collective-permute-start
  7.3 0.1 constant_dynamic-slice_fusion
  7.4 0.1 dynamic_slice.7
  7.5 0.1 copy.19
  7.6 0.1 iota_compare_fusion
  7.7 0.1 broadcast_add_fusion
  7.7 0.3 and_reduce_fusion
  8.0 0.1 copy.20
  8.1 0.6 broadcast_select_fusion.dead
  8.7 1.6 %collective-permute-done.halo = bf16[512,1024]{1,0:T(8,128)(2,1)} collective-permute-done((bf16[512,1024]{1,0:T(8,128)(2,1)}, bf16[512,1024]{1,0:T(8,128)(2,1)}, u32[]{:S(2)}, u32[]{:S(2)}) %collective-permute-start) | collective-permute-done | bytes 1048608 | tf_op jit(solution)/shard_map/ppermute | solution.py:340
  10.3 12.7 %edge_tiles.3 = (bf16[768,1024]{1,0:T(8,128)(2,1)}, bf16[512,1024]{1,0:T(8,128)(2,1)}, bf16[512,1024]{1,0:T(8,128)(2,1)}, bf16[512,1024]{1,0:T(8,128)(2,1)}) custom-call(s32[1]{0:T(128)} %bitcast.1.place, f32[6,5]{1,0:T(8,128)} %broadcast_select_fusion.dead, bf16[768,1024]{1,0:T(8,128)(2,1)} %q.7, bf16[768,1024]{1,0:T(8,128)(2,1)} %do.7, ...), custom_call_target="tpu_custom_call" | custom-call | flops 1 | bytes 1 | tf_op jit(solution)/shard_map/edge_tiles/pallas_call | solution.py:367
  23.0 0.2 collective-permute-start.3
  23.2 3.4 %collective-permute-start.1 = (bf16[512,512]{1,0:T(8,128)(2,1)}, bf16[512,512]{1,0:T(8,128)(2,1)}, u32[]{:S(2)}, u32[]{:S(2)}) collective-permute-start(bf16[512,512]{1,0:T(8,128)(2,1)} %get-tuple-element.28), channel_id=1, source_target_pairs={{1,2},{3,4},{5,6},{7,8},{9,10},{11,12},{13,14},{2,1},{4,3},{6,5},{... | collective-permute-start | bytes 1572872 | tf_op jit(solution)/shard_map/ppermute | solution.py:339
  26.6 7.8 %edge_tiles.4 = (bf16[768,1024]{1,0:T(8,128)(2,1)}, bf16[512,1024]{1,0:T(8,128)(2,1)}, bf16[512,1024]{1,0:T(8,128)(2,1)}, bf16[512,512]{1,0:T(8,128)(2,1)}) custom-call(s32[1]{0:T(128)} %bitcast.place, f32[6,5]{1,0:T(8,128)} %broadcast_select_fusion.dead, bf16[768,1024]{1,0:T(8,128)(2,1)} %q.7, ...), custom_call_target="tpu_custom_call", output_to_operand_aliasing={{0}: (9, {})} | custom-call | flops 1 | bytes 1 | tf_op jit(solution)/shard_map/edge_tiles/pallas_call | solution.py:367
  34.4 2.1 %collective-permute-start.4 = (bf16[512,512]{1,0:T(8,128)(2,1)}, bf16[512,512]{1,0:T(8,128)(2,1)}, u32[]{:S(2)}, u32[]{:S(2)}) collective-permute-start(bf16[512,512]{1,0:T(8,128)(2,1)} %get-tuple-element.41), channel_id=1, source_target_pairs={{1,2},{3,4},{5,6},{7,8},{9,10},{11,12},{13,14},{2,1},{4,3},{6,5},{... | collective-permute-start | bytes 1572872 | tf_op jit(solution)/shard_map/ppermute | solution.py:397
  36.6 3.0 %collective-permute-done.1.halo = bf16[512,512]{1,0:T(8,128)(2,1)} collective-permute-done((bf16[512,512]{1,0:T(8,128)(2,1)}, bf16[512,512]{1,0:T(8,128)(2,1)}, u32[]{:S(2)}, u32[]{:S(2)}) %collective-permute-start.1) | collective-permute-done | bytes 524320 | tf_op jit(solution)/shard_map/ppermute | solution.py:339
  39.6 7.8 %edge_tiles.5 = (bf16[768,1024]{1,0:T(8,128)(2,1)}, bf16[512,1024]{1,0:T(8,128)(2,1)}, bf16[512,1024]{1,0:T(8,128)(2,1)}, bf16[512,512]{1,0:T(8,128)(2,1)}) custom-call(s32[1]{0:T(128)} %bitcast.place, f32[6,5]{1,0:T(8,128)} %broadcast_select_fusion.dead, bf16[768,1024]{1,0:T(8,128)(2,1)} %q.7, ...), custom_call_target="tpu_custom_call", output_to_operand_aliasing={{0}: (9, {}), {1}: (10, {}), {2}: (11, {})} | custom-call | flops 1 | bytes 1 | tf_op jit(solution)/shard_map/edge_tiles/pallas_call | solution.py:367
  47.4 3.4 %collective-permute-start.5 = (bf16[512,512]{1,0:T(8,128)(2,1)}, bf16[512,512]{1,0:T(8,128)(2,1)}, u32[]{:S(2)}, u32[]{:S(2)}) collective-permute-start(bf16[512,512]{1,0:T(8,128)(2,1)} %get-tuple-element.44), channel_id=1, source_target_pairs={{1,2},{3,4},{5,6},{7,8},{9,10},{11,12},{13,14},{2,1},{4,3},{6,5},{... | collective-permute-start | bytes 1572872 | tf_op jit(solution)/shard_map/ppermute | solution.py:397
  50.8 12.8 %inner_tiles.1 = (bf16[768,1024]{1,0:T(8,128)(2,1)}, bf16[768,1024]{1,0:T(8,128)(2,1)}, bf16[768,1024]{1,0:T(8,128)(2,1)}) custom-call(s32[1]{0:T(128)} %bitcast.place, f32[6,5]{1,0:T(8,128)} %broadcast_select_fusion.dead, bf16[768,1024]{1,0:T(8,128)(2,1)} %q.7, bf16[768,1024]{1,0:T(8,128)(2,1)} %do.7, ...), custom_call_target="tpu_custom_call", output_to_operand_aliasing={{0}: (11, {})} | custom-call | flops 1 | bytes 1 | tf_op jit(solution)/shard_map/inner_tiles/pallas_call | solution.py:406
  63.6 2.1 %join_edges.2 = (bf16[768,1024]{1,0:T(8,128)(2,1)}, bf16[768,1024]{1,0:T(8,128)(2,1)}) custom-call(s32[1]{0:T(128)} %bitcast.place, bf16[768,1024]{1,0:T(8,128)(2,1)} %get-tuple-element.39.dk, bf16[768,1024]{1,0:T(8,128)(2,1)} %get-tuple-element.40.dv, bf16[512,512]{1,0:T(8,128)(2,1)} %collective-permute-done.4.back), custom_call_target="tpu_custom_call", output_to_operand_aliasing={{0}: (1, {}), {1}: (2, {})} | custom-call | flops 1 | bytes 1 | tf_op jit(solution)/shard_map/join_edges/pallas_call | solution.py:429
  65.7 2.1 %join_edges.3 = (bf16[768,1024]{1,0:T(8,128)(2,1)}, bf16[768,1024]{1,0:T(8,128)(2,1)}) custom-call(s32[1]{0:T(128)} %bitcast.place, bf16[768,1024]{1,0:T(8,128)(2,1)} %get-tuple-element.42.dk, bf16[768,1024]{1,0:T(8,128)(2,1)} %get-tuple-element.43.dv, bf16[512,512]{1,0:T(8,128)(2,1)} %collective-permute-done.5.back), custom_call_target="tpu_custom_call", output_to_operand_aliasing={{0}: (1, {}), {1}: (2, {})} | custom-call | flops 1 | bytes 1 | tf_op jit(solution)/shard_map/join_edges/pallas_call | solution.py:429
  (9 shorter events, 0.0 us)
Async XLA Ops:
  0.6 6.7 %copy-start = (s32[96,5]{0,1:T(8,128)S(1)}, s32[96,5]{0,1:T(8,128)}, u32[]{:S(2)}) copy-start(s32[96,5]{0,1:T(8,128)} %param.10) | copy-start | bytes 5764
  0.7 6.8 %copy-start.1 = (s32[96]{0:T(128)S(1)}, s32[96]{0:T(128)}, u32[]{:S(2)}) copy-start(s32[96]{0:T(128)} %param.11) | copy-start | bytes 1156
  3.5 23.0 %collective-permute-start.2 = (bf16[512,512]{1,0:T(8,128)(2,1)}, bf16[512,512]{1,0:T(8,128)(2,1)}, u32[]{:S(2)}, u32[]{:S(2)}) collective-permute-start(bf16[512,512]{1,0:T(8,128)(2,1)} %get-tuple-element.29), channel_id=1, source_target_pairs={{1,2},{3,4},{5,6},{7,8},{9,10},{11,12},{13,14},{2,1},{4,3},{6,5},{... | collective-permute-start | bytes 1572872 | tf_op jit(solution)/shard_map/ppermute | solution.py:339
  7.2 3.1 %collective-permute-start = (bf16[512,1024]{1,0:T(8,128)(2,1)}, bf16[512,1024]{1,0:T(8,128)(2,1)}, u32[]{:S(2)}, u32[]{:S(2)}) collective-permute-start(bf16[512,1024]{1,0:T(8,128)(2,1)} %get-tuple-element.25), channel_id=1, source_target_pairs={{0,1},{1,0},{2,3},{3,2},{4,5},{5,4},{6,7},{7,6},{8,9},{9,8},{10,11... | collective-permute-start | bytes 3145736 | tf_op jit(solution)/shard_map/ppermute | solution.py:340
  23.0 27.8 %collective-permute-start.3 = (bf16[512,1024]{1,0:T(8,128)(2,1)}, bf16[512,1024]{1,0:T(8,128)(2,1)}, u32[]{:S(2)}, u32[]{:S(2)}) collective-permute-start(bf16[512,1024]{1,0:T(8,128)(2,1)} %get-tuple-element.36), channel_id=1, source_target_pairs={{0,1},{1,0},{2,3},{3,2},{4,5},{5,4},{6,7},{7,6},{8,9},{9,8},{10,11... | collective-permute-start | bytes 3145736 | tf_op jit(solution)/shard_map/ppermute | solution.py:390
  23.2 16.4 %collective-permute-start.1 = (bf16[512,512]{1,0:T(8,128)(2,1)}, bf16[512,512]{1,0:T(8,128)(2,1)}, u32[]{:S(2)}, u32[]{:S(2)}) collective-permute-start(bf16[512,512]{1,0:T(8,128)(2,1)} %get-tuple-element.28), channel_id=1, source_target_pairs={{1,2},{3,4},{5,6},{7,8},{9,10},{11,12},{13,14},{2,1},{4,3},{6,5},{... | collective-permute-start | bytes 1572872 | tf_op jit(solution)/shard_map/ppermute | solution.py:339
  34.4 29.2 %collective-permute-start.4 = (bf16[512,512]{1,0:T(8,128)(2,1)}, bf16[512,512]{1,0:T(8,128)(2,1)}, u32[]{:S(2)}, u32[]{:S(2)}) collective-permute-start(bf16[512,512]{1,0:T(8,128)(2,1)} %get-tuple-element.41), channel_id=1, source_target_pairs={{1,2},{3,4},{5,6},{7,8},{9,10},{11,12},{13,14},{2,1},{4,3},{6,5},{... | collective-permute-start | bytes 1572872 | tf_op jit(solution)/shard_map/ppermute | solution.py:397
  47.4 18.3 %collective-permute-start.5 = (bf16[512,512]{1,0:T(8,128)(2,1)}, bf16[512,512]{1,0:T(8,128)(2,1)}, u32[]{:S(2)}, u32[]{:S(2)}) collective-permute-start(bf16[512,512]{1,0:T(8,128)(2,1)} %get-tuple-element.44), channel_id=1, source_target_pairs={{1,2},{3,4},{5,6},{7,8},{9,10},{11,12},{13,14},{2,1},{4,3},{6,5},{... | collective-permute-start | bytes 1572872 | tf_op jit(solution)/shard_map/ppermute | solution.py:397

commit v4 on v3

--- a/solution.py
+++ b/solution.py
@@ -260,12 +260,14 @@
 
 
 def inner_kernel(
-    group, place, dead, q, do, k, v, chip_k, chip_v, cross_k, cross_v, back, dq_in, *rest
+    group, first_steps, place, dead, q, do, k, v, chip_k, chip_v, cross_k, cross_v, back, early, dq_in, *rest
 ):
     dq, dk, dv, kt, dk_acc, dv_acc, *bufs = rest
     cross = pl.multiple_of(place[0] * BLOCK, BLOCK)
     chip = pl.multiple_of(2 * BLOCK - cross, BLOCK)
 
+
+    arrived = jnp.where(pl.program_id(0) < first_steps, 1.0, 0.0)
 
     def finish(keys, lanes):
         acc, part, other, row, out, scale = (
@@ -274,7 +276,8 @@
             else (dv_acc, chip_v, cross_v, BLOCK, dv, 1.0)
         )
         near = acc[pl.ds(cross, BLOCK), lanes] + other[:BLOCK, lanes].astype(F32)
-        out[pl.ds(cross, BLOCK), lanes] = (near * scale).astype(BF16)
+        near = near * scale + early[row : row + BLOCK, lanes].astype(F32) * arrived
+        out[pl.ds(cross, BLOCK), lanes] = near.astype(BF16)
         middle = acc[BLOCK : 2 * BLOCK, lanes] + part[BLOCK:, lanes].astype(F32)
         middle = middle + other[BLOCK:, lanes].astype(F32)
         out[BLOCK : 2 * BLOCK, lanes] = (middle * scale).astype(BF16)
@@ -285,14 +288,43 @@
     attend(group, REACH, q, do, dq, k, v, kt, dk_acc, dv_acc, dead, bufs, finish)
 
 
-def pack_kernel(place, k_cross, k_chip, v_cross, v_chip, *outs):
-    *cross_out, chip_out = outs
-    for row, cross, chip in ((0, k_cross, k_chip), (BLOCK, v_cross, v_chip)):
-        chip_out[row : row + BLOCK] = chip[...]
+class Copies:
+    def __init__(self, sems):
+        self.sems = sems
+        self.count = 0
+        self.started = {}
+
+    def start(self, piece, source, target):
+        copy = pltpu.make_async_copy(source, target, self.sems.at[self.count])
+        copy.start()
+        self.count += 1
+        self.started.setdefault(piece, []).append(copy)
+
+    def wait(self, piece):
+        for copy in self.started.pop(piece, []):
+            copy.wait()
+
+
+def pack_kernel(spans, place, keys, values, *rest):
+    *cross_out, chip_out, cross_s, chip_s, in_sems, out_sems = rest
+    cross = pl.multiple_of(place[0] * BLOCK, BLOCK)
+    chip = pl.multiple_of(2 * BLOCK - cross, BLOCK)
+    ins, outs = Copies(in_sems), Copies(out_sems)
+    for target, at in ((cross_s, cross), (chip_s, chip)):
+        for row, source in ((0, keys), (BLOCK, values)):
+            ins.start((target is cross_s, row), source.at[pl.ds(at, BLOCK)], target.at[pl.ds(row, BLOCK)])
+    for row in (0, BLOCK):
+        rows = pl.ds(row, BLOCK)
+        ins.wait((True, row))
         at = 0
-        for out in cross_out:
-            out[row : row + BLOCK] = cross[:, at : at + out.shape[1]]
-            at += out.shape[1]
+        for span, out in zip(spans, cross_out):
+            outs.start(0, cross_s.at[rows, pl.ds(at, span)], out.at[rows])
+            at += span
+    for row in (0, BLOCK):
+        rows = pl.ds(row, BLOCK)
+        ins.wait((False, row))
+        outs.start(0, chip_s.at[rows], chip_out.at[rows])
+    outs.wait(0)
 
 
 def join_kernel(place, dk, dv, back, dk_out, dv_out):
@@ -319,23 +351,29 @@
     eighth = width // CUTS[-1]
     chunks = [slice(a * eighth, b * eighth) for a, b in zip(CUTS, CUTS[1:])]
     spans = [c.stop - c.start for c in chunks]
-    cross_edge = pl.BlockSpec((BLOCK, width), lambda h, place: (place[0], 0))
-    chip_edge = pl.BlockSpec((BLOCK, width), lambda h, place: (2 - place[0], 0))
+    wide = GROUP * PAIR
+    first_steps = spans[0] // wide
+    anywhere = pl.BlockSpec(memory_space=pl.ANY)
     *cross_out, chip_out = pl.pallas_call(
-        pack_kernel,
+        functools.partial(pack_kernel, spans),
         grid_spec=pltpu.PrefetchScalarGridSpec(
             num_scalar_prefetch=1,
             grid=(1,),
-            in_specs=[cross_edge, chip_edge] * 2,
-            out_specs=[pl.BlockSpec((2 * BLOCK, span), lambda h, *_: (0, 0)) for span in spans]
-            + [pl.BlockSpec((2 * BLOCK, width), lambda h, *_: (0, 0))],
+            in_specs=[anywhere] * 2,
+            out_specs=[anywhere] * (len(spans) + 1),
+            scratch_shapes=[
+                pltpu.VMEM((2 * BLOCK, width), BF16),
+                pltpu.VMEM((2 * BLOCK, width), BF16),
+                pltpu.SemaphoreType.DMA((4,)),
+                pltpu.SemaphoreType.DMA((2 * len(spans) + 2,)),
+            ],
         ),
         out_shape=[jax.ShapeDtypeStruct((2 * BLOCK, span), BF16) for span in spans]
         + [jax.ShapeDtypeStruct((2 * BLOCK, width), BF16)],
         compiler_params=params,
         cost_estimate=cost,
         name="pack_edges",
-    )(cross_place, key_states, key_states, values, values)
+    )(cross_place, key_states, values)
     cross_halos = [lax.ppermute(x, "seq", cross_swap) for x in cross_out]
     chip_halo = lax.ppermute(chip_out, "seq", chip_swap)
 
@@ -396,21 +434,23 @@
         )
         cross_back.append(lax.ppermute(send, "seq", cross_swap))
 
-    wide = GROUP * PAIR
-
     def spec(rows, row):
         return pl.BlockSpec((rows, wide), lambda h, *_: (row, h))
 
     operands = [cross_place, dead, queries, grad_out, key_states, values]
-    operands += [chip_k, chip_v, cross_k, cross_v, chip_back, dq]
+    operands += [chip_k, chip_v, cross_k, cross_v, chip_back, cross_back[0], dq]
+    def early(h, *_):
+        return (0, jnp.minimum(h, first_steps - 1))
+
     dq, grad_keys, grad_values = pl.pallas_call(
-        functools.partial(inner_kernel, GROUP),
+        functools.partial(inner_kernel, GROUP, first_steps),
         grid_spec=pltpu.PrefetchScalarGridSpec(
             num_scalar_prefetch=2,
             grid=(width // wide,),
             in_specs=[spec(BLOCK, 1)] * 2
             + [spec(KEYS, 0)] * 2
             + [spec(2 * BLOCK, 0)] * 5
+            + [pl.BlockSpec((2 * BLOCK, wide), early)]
             + [pl.BlockSpec(memory_space=pl.ANY)],
             out_specs=[spec(BLOCK, 1), spec(KEYS, 0), spec(KEYS, 0)],
             scratch_shapes=scratch(GROUP)[2:],
@@ -422,7 +462,7 @@
         name="inner_tiles",
     )(*operands)
 
-    for c, span, back in zip(chunks, spans, cross_back):
+    for c, span, back in zip(chunks[1:], spans[1:], cross_back[1:]):
         at = c.start // span
         edge_spec = pl.BlockSpec((BLOCK, span), lambda h, place, at=at: (place[0], at))
         back_spec = pl.BlockSpec((2 * BLOCK, span), lambda h, *_: (0, 0))

time: 69 us -> 66.9 us (0.970)
  Pallas kernels: 48.1 us -> 45.9 us
    pallas_call x2 -> x1, Pallas kernels: 4.11 us -> 2.06 us  [shards(): pl.pallas_call(join_kernel, grid_spec=pltpu.PrefetchScalarGridSpec(num_sc...]
  transfers between devices with their start and end apart: 6 -> 6, of which waited for: 2 -> 2; matrix products, arithmetic and copies ran while one was open for 2% -> 2% of each run, Pallas kernels for 64% -> 63%
where the time goes in v4:
time: 66.9 us; the launch traced here: 65.6 us
  Pallas kernels  45.9 us (69%)
  starting transfers between devices  12.9 us (19%)
  waiting for transfers between devices  4.69 us (7%)
  other arithmetic  1.01 us (2%)
  between operations  0.76 us (1%)
    pallas_call x3, Pallas kernels, edge(): pl.pallas_call(functools.partial(edge_kernel, group, len(aliases)), grid_...  28.3 us
    pallas_call x1, Pallas kernels, shards(): pl.pallas_call(functools.partial(inner_kernel, GROUP, first_steps), grid_...  13.1 us
    ppermute x2, starting transfers between devices, shards(): cross_halos = [lax.ppermute(x, 'seq', cross_swap) for x in cross_out]  7.12 us
    ppermute x2, starting transfers between devices, shards(): cross_back.append(lax.ppermute(send, 'seq', cross_swap))  5.54 us
    ppermute x2, waiting for transfers between devices, shards(): cross_halos = [lax.ppermute(x, 'seq', cross_swap) for x in cross_out]  3.08 us
    pallas_call x1, Pallas kernels, shards(): pl.pallas_call(functools.partial(pack_kernel, spans), grid_spec=pltpu.Pre...  2.44 us
    pallas_call x1, Pallas kernels, shards(): pl.pallas_call(join_kernel, grid_spec=pltpu.PrefetchScalarGridSpec(num_sc...  2.06 us
    ppermute x1, waiting for transfers between devices, shards(): chip_halo = lax.ppermute(chip_out, 'seq', chip_swap)  1.6 us
  transfers between devices with their start and end apart: 6, of which 2 were waited for; matrix products, arithmetic and copies ran while one was open for 2% of the time, Pallas kernels for 63%

profile of v4, /device:TPU:17, one launch (start us, length us, event | category | flops | bytes accessed | tf_op | source)
XLA Modules:
  0.0 65.6 jit_solution(1960610721362496664)
XLA Ops:
  0.6 0.0 copy-start
  0.7 2.4 %pack_edges.1 = (bf16[512,512]{1,0:T(8,128)(2,1)}, bf16[512,512]{1,0:T(8,128)(2,1)}, bf16[512,1024]{1,0:T(8,128)(2,1)}) custom-call(s32[1]{0:T(128)} %bitcast.place, bf16[768,1024]{1,0:T(8,128)(2,1)} %k.1, bf16[768,1024]{1,0:T(8,128)(2,1)} %v.1), custom_call_target="tpu_custom_call" | custom-call | flops 1 | bytes 1 | tf_op jit(solution)/shard_map/pack_edges/pallas_call | solution.py:357
  3.1 3.7 %collective-permute-start.2 = (bf16[512,512]{1,0:T(8,128)(2,1)}, bf16[512,512]{1,0:T(8,128)(2,1)}, u32[]{:S(2)}, u32[]{:S(2)}) collective-permute-start(bf16[512,512]{1,0:T(8,128)(2,1)} %get-tuple-element.27), channel_id=1, source_target_pairs={{1,2},{3,4},{5,6},{7,8},{9,10},{11,12},{13,14},{2,1},{4,3},{6,5},{... | collective-permute-start | bytes 1572872 | tf_op jit(solution)/shard_map/ppermute | solution.py:377
  6.8 0.1 collective-permute-start
  6.9 0.1 constant_dynamic-slice_fusion
  7.0 0.1 dynamic_slice.7
  7.1 0.1 copy.17
  7.2 0.1 iota_compare_fusion
  7.3 0.1 broadcast_add_fusion
  7.3 0.3 and_reduce_fusion
  7.6 0.1 copy.18
  7.7 0.6 broadcast_select_fusion.dead
  8.3 1.6 %collective-permute-done.halo = bf16[512,1024]{1,0:T(8,128)(2,1)} collective-permute-done((bf16[512,1024]{1,0:T(8,128)(2,1)}, bf16[512,1024]{1,0:T(8,128)(2,1)}, u32[]{:S(2)}, u32[]{:S(2)}) %collective-permute-start) | collective-permute-done | bytes 1048608 | tf_op jit(solution)/shard_map/ppermute | solution.py:378
  9.9 12.7 %edge_tiles.3 = (bf16[768,1024]{1,0:T(8,128)(2,1)}, bf16[512,1024]{1,0:T(8,128)(2,1)}, bf16[512,1024]{1,0:T(8,128)(2,1)}, bf16[512,1024]{1,0:T(8,128)(2,1)}) custom-call(s32[1]{0:T(128)} %bitcast.1.place, f32[6,5]{1,0:T(8,128)} %broadcast_select_fusion.dead, bf16[768,1024]{1,0:T(8,128)(2,1)} %q.7, bf16[768,1024]{1,0:T(8,128)(2,1)} %do.7, ...), custom_call_target="tpu_custom_call" | custom-call | flops 1 | bytes 1 | tf_op jit(solution)/shard_map/edge_tiles/pallas_call | solution.py:405
  22.6 0.2 collective-permute-start.3
  22.8 3.4 %collective-permute-start.1 = (bf16[512,512]{1,0:T(8,128)(2,1)}, bf16[512,512]{1,0:T(8,128)(2,1)}, u32[]{:S(2)}, u32[]{:S(2)}) collective-permute-start(bf16[512,512]{1,0:T(8,128)(2,1)} %get-tuple-element.26), channel_id=1, source_target_pairs={{1,2},{3,4},{5,6},{7,8},{9,10},{11,12},{13,14},{2,1},{4,3},{6,5},{... | collective-permute-start | bytes 1572872 | tf_op jit(solution)/shard_map/ppermute | solution.py:377
  26.2 0.0 collective-permute-done.2.halo
  26.2 7.8 %edge_tiles.4 = (bf16[768,1024]{1,0:T(8,128)(2,1)}, bf16[512,1024]{1,0:T(8,128)(2,1)}, bf16[512,1024]{1,0:T(8,128)(2,1)}, bf16[512,512]{1,0:T(8,128)(2,1)}) custom-call(s32[1]{0:T(128)} %bitcast.place, f32[6,5]{1,0:T(8,128)} %broadcast_select_fusion.dead, bf16[768,1024]{1,0:T(8,128)(2,1)} %q.7, ...), custom_call_target="tpu_custom_call", output_to_operand_aliasing={{0}: (9, {})} | custom-call | flops 1 | bytes 1 | tf_op jit(solution)/shard_map/edge_tiles/pallas_call | solution.py:405
  34.0 2.1 %collective-permute-start.4 = (bf16[512,512]{1,0:T(8,128)(2,1)}, bf16[512,512]{1,0:T(8,128)(2,1)}, u32[]{:S(2)}, u32[]{:S(2)}) collective-permute-start(bf16[512,512]{1,0:T(8,128)(2,1)} %get-tuple-element.35), channel_id=1, source_target_pairs={{1,2},{3,4},{5,6},{7,8},{9,10},{11,12},{13,14},{2,1},{4,3},{6,5},{... | collective-permute-start | bytes 1572872 | tf_op jit(solution)/shard_map/ppermute | solution.py:435
  36.1 3.1 %collective-permute-done.1.halo = bf16[512,512]{1,0:T(8,128)(2,1)} collective-permute-done((bf16[512,512]{1,0:T(8,128)(2,1)}, bf16[512,512]{1,0:T(8,128)(2,1)}, u32[]{:S(2)}, u32[]{:S(2)}) %collective-permute-start.1) | collective-permute-done | bytes 524320 | tf_op jit(solution)/shard_map/ppermute | solution.py:377
  39.2 7.8 %edge_tiles.5 = (bf16[768,1024]{1,0:T(8,128)(2,1)}, bf16[512,1024]{1,0:T(8,128)(2,1)}, bf16[512,1024]{1,0:T(8,128)(2,1)}, bf16[512,512]{1,0:T(8,128)(2,1)}) custom-call(s32[1]{0:T(128)} %bitcast.place, f32[6,5]{1,0:T(8,128)} %broadcast_select_fusion.dead, bf16[768,1024]{1,0:T(8,128)(2,1)} %q.7, ...), custom_call_target="tpu_custom_call", output_to_operand_aliasing={{0}: (9, {}), {1}: (10, {}), {2}: (11, {})} | custom-call | flops 1 | bytes 1 | tf_op jit(solution)/shard_map/edge_tiles/pallas_call | solution.py:405
  47.0 3.4 %collective-permute-start.5 = (bf16[512,512]{1,0:T(8,128)(2,1)}, bf16[512,512]{1,0:T(8,128)(2,1)}, u32[]{:S(2)}, u32[]{:S(2)}) collective-permute-start(bf16[512,512]{1,0:T(8,128)(2,1)} %get-tuple-element.40), channel_id=1, source_target_pairs={{1,2},{3,4},{5,6},{7,8},{9,10},{11,12},{13,14},{2,1},{4,3},{6,5},{... | collective-permute-start | bytes 1572872 | tf_op jit(solution)/shard_map/ppermute | solution.py:435
  50.5 13.1 %inner_tiles.1 = (bf16[768,1024]{1,0:T(8,128)(2,1)}, bf16[768,1024]{1,0:T(8,128)(2,1)}, bf16[768,1024]{1,0:T(8,128)(2,1)}) custom-call(s32[1]{0:T(128)} %bitcast.place, f32[6,5]{1,0:T(8,128)} %broadcast_select_fusion.dead, bf16[768,1024]{1,0:T(8,128)(2,1)} %q.7, bf16[768,1024]{1,0:T(8,128)(2,1)} %do.7, ...), custom_call_target="tpu_custom_call", output_to_operand_aliasing={{0}: (12, {})} | custom-call | flops 1 | bytes 1 | tf_op jit(solution)/shard_map/inner_tiles/pallas_call | solution.py:445
  63.5 2.1 %join_edges.1 = (bf16[768,1024]{1,0:T(8,128)(2,1)}, bf16[768,1024]{1,0:T(8,128)(2,1)}) custom-call(s32[1]{0:T(128)} %bitcast.place, bf16[768,1024]{1,0:T(8,128)(2,1)} %get-tuple-element.38.dk, bf16[768,1024]{1,0:T(8,128)(2,1)} %get-tuple-element.39.dv, bf16[512,512]{1,0:T(8,128)(2,1)} %collective-permute-done.5.back), custom_call_target="tpu_custom_call", output_to_operand_aliasing={{0}: (1, {}), {1}: (2, {})} | custom-call | flops 1 | bytes 1 | tf_op jit(solution)/shard_map/join_edges/pallas_call | solution.py:469
  (8 shorter events, 0.0 us)
Async XLA Ops:
  0.6 6.3 %copy-start = (s32[96,5]{0,1:T(8,128)S(1)}, s32[96,5]{0,1:T(8,128)}, u32[]{:S(2)}) copy-start(s32[96,5]{0,1:T(8,128)} %param.10) | copy-start | bytes 5764
  0.7 6.4 %copy-start.1 = (s32[96]{0:T(128)S(1)}, s32[96]{0:T(128)}, u32[]{:S(2)}) copy-start(s32[96]{0:T(128)} %param.11) | copy-start | bytes 1156
  3.1 23.1 %collective-permute-start.2 = (bf16[512,512]{1,0:T(8,128)(2,1)}, bf16[512,512]{1,0:T(8,128)(2,1)}, u32[]{:S(2)}, u32[]{:S(2)}) collective-permute-start(bf16[512,512]{1,0:T(8,128)(2,1)} %get-tuple-element.27), channel_id=1, source_target_pairs={{1,2},{3,4},{5,6},{7,8},{9,10},{11,12},{13,14},{2,1},{4,3},{6,5},{... | collective-permute-start | bytes 1572872 | tf_op jit(solution)/shard_map/ppermute | solution.py:377
  6.8 3.1 %collective-permute-start = (bf16[512,1024]{1,0:T(8,128)(2,1)}, bf16[512,1024]{1,0:T(8,128)(2,1)}, u32[]{:S(2)}, u32[]{:S(2)}) collective-permute-start(bf16[512,1024]{1,0:T(8,128)(2,1)} %get-tuple-element.23), channel_id=1, source_target_pairs={{0,1},{1,0},{2,3},{3,2},{4,5},{5,4},{6,7},{7,6},{8,9},{9,8},{10,11... | collective-permute-start | bytes 3145736 | tf_op jit(solution)/shard_map/ppermute | solution.py:378
  22.6 27.9 %collective-permute-start.3 = (bf16[512,1024]{1,0:T(8,128)(2,1)}, bf16[512,1024]{1,0:T(8,128)(2,1)}, u32[]{:S(2)}, u32[]{:S(2)}) collective-permute-start(bf16[512,1024]{1,0:T(8,128)(2,1)} %get-tuple-element.34), channel_id=1, source_target_pairs={{0,1},{1,0},{2,3},{3,2},{4,5},{5,4},{6,7},{7,6},{8,9},{9,8},{10,11... | collective-permute-start | bytes 3145736 | tf_op jit(solution)/shard_map/ppermute | solution.py:428
  22.8 16.4 %collective-permute-start.1 = (bf16[512,512]{1,0:T(8,128)(2,1)}, bf16[512,512]{1,0:T(8,128)(2,1)}, u32[]{:S(2)}, u32[]{:S(2)}) collective-permute-start(bf16[512,512]{1,0:T(8,128)(2,1)} %get-tuple-element.26), channel_id=1, source_target_pairs={{1,2},{3,4},{5,6},{7,8},{9,10},{11,12},{13,14},{2,1},{4,3},{6,5},{... | collective-permute-start | bytes 1572872 | tf_op jit(solution)/shard_map/ppermute | solution.py:377
  34.0 16.5 %collective-permute-start.4 = (bf16[512,512]{1,0:T(8,128)(2,1)}, bf16[512,512]{1,0:T(8,128)(2,1)}, u32[]{:S(2)}, u32[]{:S(2)}) collective-permute-start(bf16[512,512]{1,0:T(8,128)(2,1)} %get-tuple-element.35), channel_id=1, source_target_pairs={{1,2},{3,4},{5,6},{7,8},{9,10},{11,12},{13,14},{2,1},{4,3},{6,5},{... | collective-permute-start | bytes 1572872 | tf_op jit(solution)/shard_map/ppermute | solution.py:435
  47.0 16.5 %collective-permute-start.5 = (bf16[512,512]{1,0:T(8,128)(2,1)}, bf16[512,512]{1,0:T(8,128)(2,1)}, u32[]{:S(2)}, u32[]{:S(2)}) collective-permute-start(bf16[512,512]{1,0:T(8,128)(2,1)} %get-tuple-element.40), channel_id=1, source_target_pairs={{1,2},{3,4},{5,6},{7,8},{9,10},{11,12},{13,14},{2,1},{4,3},{6,5},{... | collective-permute-start | bytes 1572872 | tf_op jit(solution)/shard_map/ppermute | solution.py:435

commit v5 on v4

--- a/solution.py
+++ b/solution.py
@@ -209,8 +209,11 @@
         if 0 <= step - 2 < count:
             late += query_grads(step - 2)
         g, odd = divmod(step - 3, 2)
-        if 0 <= g < pairs_here:
+        last = g == pairs_here - 1
+        if 0 <= g < pairs_here and not (odd and last):
             late += key_grads(g, *((ds_buf, qw, dk_acc) if odd else (e_buf, dw, dv_acc)))
+        if last and not odd:
+            late += key_grads(g, ds_buf, qw, dk_acc)
         merge(
             scores(step) if step < count else [],
             softmax(step - 1) if 0 <= step - 1 < count else [],
@@ -235,32 +238,31 @@
     ]
 
 
-def edge_kernel(group, chained, place, dead, q, do, k_near, k_mid, v_near, v_mid, halo, *rest):
+def edge_kernel(group, chained, place, dead, q, do, k, v, halo, *rest):
     rest = rest[chained:]
-    dq, part_k, part_v, send, k_ext, v_ext, kt, dk_acc, dv_acc, *bufs = rest
+    dq, part, send, k_ext, v_ext, kt, dk_acc, dv_acc, *bufs = rest
     low_edge = place[0] == 0
     outside = pl.multiple_of(jnp.where(low_edge, 0, 2 * BLOCK), BLOCK)
     inside = pl.multiple_of(jnp.where(low_edge, 2 * BLOCK, 0), BLOCK)
-
-    for row, near, mid, ext in ((0, k_near, k_mid, k_ext), (BLOCK, v_near, v_mid, v_ext)):
+    held = pl.multiple_of(jnp.where(low_edge, BLOCK, 0), BLOCK)
+
+    for row, own, ext in ((0, k, k_ext), (BLOCK, v, v_ext)):
         ext[pl.ds(outside, BLOCK)] = halo[row : row + BLOCK]
-        ext[BLOCK : 2 * BLOCK] = near[...]
-        ext[pl.ds(inside, BLOCK)] = mid[...]
+        ext[pl.ds(held, 2 * BLOCK)] = own[...]
 
     def finish(keys, lanes):
-        acc, part, row, scale = (
-            (dk_acc, part_k, 0, SCALE) if keys else (dv_acc, part_v, BLOCK, 1.0)
-        )
+        acc, row, scale = (dk_acc, 0, SCALE) if keys else (dv_acc, BLOCK, 1.0)
         send[row : row + BLOCK, lanes] = (acc[pl.ds(outside, BLOCK), lanes] * scale).astype(BF16)
-        part[:BLOCK, lanes] = acc[BLOCK : 2 * BLOCK, lanes].astype(BF16)
-        part[BLOCK:, lanes] = acc[pl.ds(inside, BLOCK), lanes].astype(BF16)
+        near, mid = slice(2 * row, 2 * row + BLOCK), slice(2 * row + BLOCK, 2 * row + 2 * BLOCK)
+        part[near, lanes] = acc[BLOCK : 2 * BLOCK, lanes].astype(BF16)
+        part[mid, lanes] = acc[pl.ds(inside, BLOCK), lanes].astype(BF16)
 
     base = place[0] * REACH
     attend(group, base, q, do, dq, k_ext, v_ext, kt, dk_acc, dv_acc, dead, bufs, finish)
 
 
 def inner_kernel(
-    group, first_steps, place, dead, q, do, k, v, chip_k, chip_v, cross_k, cross_v, back, early, dq_in, *rest
+    group, first_steps, place, dead, q, do, k, v, chip_part, cross_part, back, early, dq_in, *rest
 ):
     dq, dk, dv, kt, dk_acc, dv_acc, *bufs = rest
     cross = pl.multiple_of(place[0] * BLOCK, BLOCK)
@@ -270,11 +272,9 @@
     arrived = jnp.where(pl.program_id(0) < first_steps, 1.0, 0.0)
 
     def finish(keys, lanes):
-        acc, part, other, row, out, scale = (
-            (dk_acc, chip_k, cross_k, 0, dk, SCALE)
-            if keys
-            else (dv_acc, chip_v, cross_v, BLOCK, dv, 1.0)
-        )
+        acc, row, out, scale = (dk_acc, 0, dk, SCALE) if keys else (dv_acc, BLOCK, dv, 1.0)
+        rows = pl.ds(2 * row, 2 * BLOCK)
+        part, other = chip_part.at[rows], cross_part.at[rows]
         near = acc[pl.ds(cross, BLOCK), lanes] + other[:BLOCK, lanes].astype(F32)
         near = near * scale + early[row : row + BLOCK, lanes].astype(F32) * arrived
         out[pl.ds(cross, BLOCK), lanes] = near.astype(BF16)
@@ -378,25 +378,24 @@
     chip_halo = lax.ppermute(chip_out, "seq", chip_swap)
 
     def edge(place, halo, column, lanes, earlier):
-        group = min(GROUP, lanes // PAIR)
+        group = 2 * GROUP if earlier[0] is None else GROUP
         wide = group * PAIR
         at = column // wide
 
         def near(h, place, *_):
             return (place[0], at + h)
 
-        def mid(h, *_):
-            return (1, at + h)
+        def window(h, place, *_):
+            return (place[0] // 2 * BLOCK, (at + h) * wide)
 
         def own(h, *_):
             return (0, h)
 
         one = pl.BlockSpec((BLOCK, wide), near)
-        two = pl.BlockSpec((BLOCK, wide), mid)
+        two = pl.BlockSpec((pl.Element(2 * BLOCK), pl.Element(wide)), window)
         double = pl.BlockSpec((2 * BLOCK, wide), own)
-        wide_double = pl.BlockSpec((2 * BLOCK, wide), lambda h, *_: (0, at + h))
-        operands = [place, dead, queries, grad_out, key_states, key_states]
-        operands += [values, values, halo]
+        wide_part = pl.BlockSpec((4 * BLOCK, wide), lambda h, *_: (0, at + h))
+        operands = [place, dead, queries, grad_out, key_states, values, halo]
         aliases = {}
         for i, array in enumerate(earlier):
             if array is not None:
@@ -407,15 +406,14 @@
             grid_spec=pltpu.PrefetchScalarGridSpec(
                 num_scalar_prefetch=2,
                 grid=(lanes // wide,),
-                in_specs=[one, one, one, two, one, two, double]
+                in_specs=[one, one, two, two, double]
                 + [pl.BlockSpec(memory_space=pl.ANY)] * len(aliases),
-                out_specs=[one, wide_double, wide_double, double],
+                out_specs=[one, wide_part, double],
                 scratch_shapes=scratch(group),
             ),
             out_shape=[
                 jax.ShapeDtypeStruct((rows_dev, width), BF16),
-                jax.ShapeDtypeStruct((2 * BLOCK, width), BF16),
-                jax.ShapeDtypeStruct((2 * BLOCK, width), BF16),
+                jax.ShapeDtypeStruct((4 * BLOCK, width), BF16),
                 jax.ShapeDtypeStruct((2 * BLOCK, lanes), BF16),
             ],
             input_output_aliases=aliases,
@@ -424,13 +422,13 @@
             name="edge_tiles",
         )(*operands)
 
-    dq, chip_k, chip_v, chip_send = edge(chip_place, chip_halo, 0, width, [None] * 3)
+    dq, chip_part, chip_send = edge(chip_place, chip_halo, 0, width, [None] * 2)
     chip_back = lax.ppermute(chip_send, "seq", chip_swap)
-    cross_k = cross_v = None
+    cross_part = None
     cross_back = []
     for c, halo in zip(chunks, cross_halos):
-        dq, cross_k, cross_v, send = edge(
-            cross_place, halo, c.start, c.stop - c.start, [dq, cross_k, cross_v]
+        dq, cross_part, send = edge(
+            cross_place, halo, c.start, c.stop - c.start, [dq, cross_part]
         )
         cross_back.append(lax.ppermute(send, "seq", cross_swap))
 
@@ -438,7 +436,7 @@
         return pl.BlockSpec((rows, wide), lambda h, *_: (row, h))
 
     operands = [cross_place, dead, queries, grad_out, key_states, values]
-    operands += [chip_k, chip_v, cross_k, cross_v, chip_back, cross_back[0], dq]
+    operands += [chip_part, cross_part, chip_back, cross_back[0], dq]
     def early(h, *_):
         return (0, jnp.minimum(h, first_steps - 1))
 
@@ -449,7 +447,8 @@
             grid=(width // wide,),
             in_specs=[spec(BLOCK, 1)] * 2
             + [spec(KEYS, 0)] * 2
-            + [spec(2 * BLOCK, 0)] * 5
+            + [spec(4 * BLOCK, 0)] * 2
+            + [spec(2 * BLOCK, 0)]
             + [pl.BlockSpec((2 * BLOCK, wide), early)]
             + [pl.BlockSpec(memory_space=pl.ANY)],
             out_specs=[spec(BLOCK, 1), spec(KEYS, 0), spec(KEYS, 0)],

time: 66.9 us -> 71.4 us (1.067); the launches traced: 65.6 us -> 71 us
  waiting for transfers between devices: 4.69 us -> 10.1 us
    ppermute x2, waiting for transfers between devices: 0.01 us -> 3.78 us  [shards(): cross_back.append(lax.ppermute(send, 'seq', cross_swap))]
    ppermute x2, waiting for transfers between devices: 3.08 us -> 5.08 us  [shards(): cross_halos = [lax.ppermute(x, 'seq', cross_swap) for x in cross_out]]
    ppermute x1, starting transfers between devices: 0.07 us -> 1.57 us  [shards(): chip_halo = lax.ppermute(chip_out, 'seq', chip_swap)]
    ppermute x2, starting transfers between devices: 7.12 us -> 5.63 us  [shards(): cross_halos = [lax.ppermute(x, 'seq', cross_swap) for x in cross_out]]
  transfers between devices with their start and end apart: 6 -> 6, of which waited for: 2 -> 3; matrix products, arithmetic and copies ran while one was open for 2% -> 2% of each run, Pallas kernels for 63% -> 58%
where the time goes in v5:
time: 71.4 us; the launch traced here: 71 us
  Pallas kernels  45.4 us (64%)
  starting transfers between devices  13.3 us (19%)
  waiting for transfers between devices  10.1 us (14%)
  other arithmetic  1.01 us (1%)
  between operations  0.72 us (1%)
    pallas_call x3, Pallas kernels, edge(): pl.pallas_call(functools.partial(edge_kernel, group, len(aliases)), grid_...  27.8 us
    pallas_call x1, Pallas kernels, shards(): pl.pallas_call(functools.partial(inner_kernel, GROUP, first_steps), grid_...  13 us
    ppermute x2, starting transfers between devices, shards(): cross_back.append(lax.ppermute(send, 'seq', cross_swap))  5.73 us
    ppermute x2, starting transfers between devices, shards(): cross_halos = [lax.ppermute(x, 'seq', cross_swap) for x in cross_out]  5.63 us
    ppermute x2, waiting for transfers between devices, shards(): cross_halos = [lax.ppermute(x, 'seq', cross_swap) for x in cross_out]  5.08 us
    ppermute x2, waiting for transfers between devices, shards(): cross_back.append(lax.ppermute(send, 'seq', cross_swap))  3.78 us
    pallas_call x1, Pallas kernels, shards(): pl.pallas_call(functools.partial(pack_kernel, spans), grid_spec=pltpu.Pre...  2.44 us
    pallas_call x1, Pallas kernels, shards(): pl.pallas_call(join_kernel, grid_spec=pltpu.PrefetchScalarGridSpec(num_sc...  2.06 us
  transfers between devices with their start and end apart: 6, of which 3 were waited for; matrix products, arithmetic and copies ran while one was open for 2% of the time, Pallas kernels for 58%

profile of v5, /device:TPU:17, one launch (start us, length us, event | category | flops | bytes accessed | tf_op | source)
XLA Modules:
  0.0 71.0 jit_solution(15152271513459746772)
XLA Ops:
  0.6 0.0 copy-start
  0.7 2.4 %pack_edges.1 = (bf16[512,512]{1,0:T(8,128)(2,1)}, bf16[512,512]{1,0:T(8,128)(2,1)}, bf16[512,1024]{1,0:T(8,128)(2,1)}) custom-call(s32[1]{0:T(128)} %bitcast.place, bf16[768,1024]{1,0:T(8,128)(2,1)} %k.7, bf16[768,1024]{1,0:T(8,128)(2,1)} %v.7), custom_call_target="tpu_custom_call" | custom-call | flops 1 | bytes 1 | tf_op jit(solution)/shard_map/pack_edges/pallas_call | solution.py:357
  3.1 3.7 %collective-permute-start.1 = (bf16[512,512]{1,0:T(8,128)(2,1)}, bf16[512,512]{1,0:T(8,128)(2,1)}, u32[]{:S(2)}, u32[]{:S(2)}) collective-permute-start(bf16[512,512]{1,0:T(8,128)(2,1)} %get-tuple-element.22), channel_id=1, source_target_pairs={{1,2},{3,4},{5,6},{7,8},{9,10},{11,12},{13,14},{2,1},{4,3},{6,5},{... | collective-permute-start | bytes 1572872 | tf_op jit(solution)/shard_map/ppermute | solution.py:377
  6.8 1.9 %collective-permute-start.2 = (bf16[512,512]{1,0:T(8,128)(2,1)}, bf16[512,512]{1,0:T(8,128)(2,1)}, u32[]{:S(2)}, u32[]{:S(2)}) collective-permute-start(bf16[512,512]{1,0:T(8,128)(2,1)} %get-tuple-element.23), channel_id=1, source_target_pairs={{1,2},{3,4},{5,6},{7,8},{9,10},{11,12},{13,14},{2,1},{4,3},{6,5},{... | collective-permute-start | bytes 1572872 | tf_op jit(solution)/shard_map/ppermute | solution.py:377
  8.8 1.6 %collective-permute-start = (bf16[512,1024]{1,0:T(8,128)(2,1)}, bf16[512,1024]{1,0:T(8,128)(2,1)}, u32[]{:S(2)}, u32[]{:S(2)}) collective-permute-start(bf16[512,1024]{1,0:T(8,128)(2,1)} %get-tuple-element.20), channel_id=1, source_target_pairs={{0,1},{1,0},{2,3},{3,2},{4,5},{5,4},{6,7},{7,6},{8,9},{9,8},{10,11... | collective-permute-start | bytes 3145736 | tf_op jit(solution)/shard_map/ppermute | solution.py:378
  10.3 0.1 constant_dynamic-slice_fusion
  10.4 0.1 dynamic_slice.7
  10.5 0.1 copy.16
  10.6 0.1 iota_compare_fusion
  10.7 0.1 broadcast_add_fusion
  10.7 0.3 and_reduce_fusion
  11.0 0.1 copy.17
  11.1 0.6 broadcast_select_fusion.dead
  11.7 1.3 %collective-permute-done.halo = bf16[512,1024]{1,0:T(8,128)(2,1)} collective-permute-done((bf16[512,1024]{1,0:T(8,128)(2,1)}, bf16[512,1024]{1,0:T(8,128)(2,1)}, u32[]{:S(2)}, u32[]{:S(2)}) %collective-permute-start) | collective-permute-done | bytes 1048608 | tf_op jit(solution)/shard_map/ppermute | solution.py:378
  13.0 12.4 %edge_tiles.3 = (bf16[768,1024]{1,0:T(8,128)(2,1)}, bf16[1024,1024]{1,0:T(8,128)(2,1)}, bf16[512,1024]{1,0:T(8,128)(2,1)}) custom-call(s32[1]{0:T(128)} %bitcast.1.place, f32[6,5]{1,0:T(8,128)} %broadcast_select_fusion.dead, bf16[768,1024]{1,0:T(8,128)(2,1)} %q.7, bf16[768,1024]{1,0:T(8,128)(2,1)} %do.7, bf16[768,1024]{1,0:T(8,128)(2,1)} %k.7, ...), custom_call_target="tpu_custom_call" | custom-call | flops 1 | bytes 1 | tf_op jit(solution)/shard_map/edge_tiles/pallas_call | solution.py:404
  25.4 0.4 collective-permute-start.3
  25.8 5.1 %collective-permute-done.2.halo = bf16[512,512]{1,0:T(8,128)(2,1)} collective-permute-done((bf16[512,512]{1,0:T(8,128)(2,1)}, bf16[512,512]{1,0:T(8,128)(2,1)}, u32[]{:S(2)}, u32[]{:S(2)}) %collective-permute-start.2) | collective-permute-done | bytes 524320 | tf_op jit(solution)/shard_map/ppermute | solution.py:377
  30.9 7.7 %edge_tiles.4 = (bf16[768,1024]{1,0:T(8,128)(2,1)}, bf16[1024,1024]{1,0:T(8,128)(2,1)}, bf16[512,512]{1,0:T(8,128)(2,1)}) custom-call(s32[1]{0:T(128)} %bitcast.place, f32[6,5]{1,0:T(8,128)} %broadcast_select_fusion.dead, bf16[768,1024]{1,0:T(8,128)(2,1)} %q.7, bf16[768,1024]{1,0:T(8,128)(2,1)} %do.7, ...), custom_call_target="tpu_custom_call", output_to_operand_aliasing={{0}: (7, {})} | custom-call | flops 1 | bytes 1 | tf_op jit(solution)/shard_map/edge_tiles/pallas_call | solution.py:404
  38.6 3.6 %collective-permute-start.4 = (bf16[512,512]{1,0:T(8,128)(2,1)}, bf16[512,512]{1,0:T(8,128)(2,1)}, u32[]{:S(2)}, u32[]{:S(2)}) collective-permute-start(bf16[512,512]{1,0:T(8,128)(2,1)} %get-tuple-element.29), channel_id=1, source_target_pairs={{1,2},{3,4},{5,6},{7,8},{9,10},{11,12},{13,14},{2,1},{4,3},{6,5},{... | collective-permute-start | bytes 1572872 | tf_op jit(solution)/shard_map/ppermute | solution.py:433
  42.2 7.7 %edge_tiles.5 = (bf16[768,1024]{1,0:T(8,128)(2,1)}, bf16[1024,1024]{1,0:T(8,128)(2,1)}, bf16[512,512]{1,0:T(8,128)(2,1)}) custom-call(s32[1]{0:T(128)} %bitcast.place, f32[6,5]{1,0:T(8,128)} %broadcast_select_fusion.dead, bf16[768,1024]{1,0:T(8,128)(2,1)} %q.7, bf16[768,1024]{1,0:T(8,128)(2,1)} %do.7, ...), custom_call_target="tpu_custom_call", output_to_operand_aliasing={{0}: (7, {}), {1}: (8, {})} | custom-call | flops 1 | bytes 1 | tf_op jit(solution)/shard_map/edge_tiles/pallas_call | solution.py:404
  50.0 2.1 %collective-permute-start.5 = (bf16[512,512]{1,0:T(8,128)(2,1)}, bf16[512,512]{1,0:T(8,128)(2,1)}, u32[]{:S(2)}, u32[]{:S(2)}) collective-permute-start(bf16[512,512]{1,0:T(8,128)(2,1)} %get-tuple-element.34), channel_id=1, source_target_pairs={{1,2},{3,4},{5,6},{7,8},{9,10},{11,12},{13,14},{2,1},{4,3},{6,5},{... | collective-permute-start | bytes 1572872 | tf_op jit(solution)/shard_map/ppermute | solution.py:433
  52.1 3.8 %collective-permute-done.4.early = bf16[512,512]{1,0:T(8,128)(2,1)} collective-permute-done((bf16[512,512]{1,0:T(8,128)(2,1)}, bf16[512,512]{1,0:T(8,128)(2,1)}, u32[]{:S(2)}, u32[]{:S(2)}) %collective-permute-start.4) | collective-permute-done | bytes 524320 | tf_op jit(solution)/shard_map/ppermute | solution.py:433
  55.9 13.0 %inner_tiles.1 = (bf16[768,1024]{1,0:T(8,128)(2,1)}, bf16[768,1024]{1,0:T(8,128)(2,1)}, bf16[768,1024]{1,0:T(8,128)(2,1)}) custom-call(s32[1]{0:T(128)} %bitcast.place, f32[6,5]{1,0:T(8,128)} %broadcast_select_fusion.dead, bf16[768,1024]{1,0:T(8,128)(2,1)} %q.7, bf16[768,1024]{1,0:T(8,128)(2,1)} %do.7, ...), custom_call_target="tpu_custom_call", output_to_operand_aliasing={{0}: (10, {})} | custom-call | flops 1 | bytes 1 | tf_op jit(solution)/shard_map/inner_tiles/pallas_call | solution.py:443
  68.9 2.1 %join_edges.1 = (bf16[768,1024]{1,0:T(8,128)(2,1)}, bf16[768,1024]{1,0:T(8,128)(2,1)}) custom-call(s32[1]{0:T(128)} %bitcast.place, bf16[768,1024]{1,0:T(8,128)(2,1)} %get-tuple-element.32.dk, bf16[768,1024]{1,0:T(8,128)(2,1)} %get-tuple-element.33.dv, bf16[512,512]{1,0:T(8,128)(2,1)} %collective-permute-done.5.back), custom_call_target="tpu_custom_call", output_to_operand_aliasing={{0}: (1, {}), {1}: (2, {})} | custom-call | flops 1 | bytes 1 | tf_op jit(solution)/shard_map/join_edges/pallas_call | solution.py:468
  (8 shorter events, 0.0 us)
Async XLA Ops:
  0.6 9.7 %copy-start = (s32[96,5]{0,1:T(8,128)S(1)}, s32[96,5]{0,1:T(8,128)}, u32[]{:S(2)}) copy-start(s32[96,5]{0,1:T(8,128)} %param.10) | copy-start | bytes 5764
  0.7 9.8 %copy-start.1 = (s32[96]{0:T(128)S(1)}, s32[96]{0:T(128)}, u32[]{:S(2)}) copy-start(s32[96]{0:T(128)} %param.11) | copy-start | bytes 1156
  3.1 39.1 %collective-permute-start.1 = (bf16[512,512]{1,0:T(8,128)(2,1)}, bf16[512,512]{1,0:T(8,128)(2,1)}, u32[]{:S(2)}, u32[]{:S(2)}) collective-permute-start(bf16[512,512]{1,0:T(8,128)(2,1)} %get-tuple-element.22), channel_id=1, source_target_pairs={{1,2},{3,4},{5,6},{7,8},{9,10},{11,12},{13,14},{2,1},{4,3},{6,5},{... | collective-permute-start | bytes 1572872 | tf_op jit(solution)/shard_map/ppermute | solution.py:377
  6.8 24.0 %collective-permute-start.2 = (bf16[512,512]{1,0:T(8,128)(2,1)}, bf16[512,512]{1,0:T(8,128)(2,1)}, u32[]{:S(2)}, u32[]{:S(2)}) collective-permute-start(bf16[512,512]{1,0:T(8,128)(2,1)} %get-tuple-element.23), channel_id=1, source_target_pairs={{1,2},{3,4},{5,6},{7,8},{9,10},{11,12},{13,14},{2,1},{4,3},{6,5},{... | collective-permute-start | bytes 1572872 | tf_op jit(solution)/shard_map/ppermute | solution.py:377
  8.8 4.2 %collective-permute-start = (bf16[512,1024]{1,0:T(8,128)(2,1)}, bf16[512,1024]{1,0:T(8,128)(2,1)}, u32[]{:S(2)}, u32[]{:S(2)}) collective-permute-start(bf16[512,1024]{1,0:T(8,128)(2,1)} %get-tuple-element.20), channel_id=1, source_target_pairs={{0,1},{1,0},{2,3},{3,2},{4,5},{5,4},{6,7},{7,6},{8,9},{9,8},{10,11... | collective-permute-start | bytes 3145736 | tf_op jit(solution)/shard_map/ppermute | solution.py:378
  25.4 30.5 %collective-permute-start.3 = (bf16[512,1024]{1,0:T(8,128)(2,1)}, bf16[512,1024]{1,0:T(8,128)(2,1)}, u32[]{:S(2)}, u32[]{:S(2)}) collective-permute-start(bf16[512,1024]{1,0:T(8,128)(2,1)} %get-tuple-element.28), channel_id=1, source_target_pairs={{0,1},{1,0},{2,3},{3,2},{4,5},{5,4},{6,7},{7,6},{8,9},{9,8},{10,11... | collective-permute-start | bytes 3145736 | tf_op jit(solution)/shard_map/ppermute | solution.py:426
  38.6 17.3 %collective-permute-start.4 = (bf16[512,512]{1,0:T(8,128)(2,1)}, bf16[512,512]{1,0:T(8,128)(2,1)}, u32[]{:S(2)}, u32[]{:S(2)}) collective-permute-start(bf16[512,512]{1,0:T(8,128)(2,1)} %get-tuple-element.29), channel_id=1, source_target_pairs={{1,2},{3,4},{5,6},{7,8},{9,10},{11,12},{13,14},{2,1},{4,3},{6,5},{... | collective-permute-start | bytes 1572872 | tf_op jit(solution)/shard_map/ppermute | solution.py:433
  50.0 18.9 %collective-permute-start.5 = (bf16[512,512]{1,0:T(8,128)(2,1)}, bf16[512,512]{1,0:T(8,128)(2,1)}, u32[]{:S(2)}, u32[]{:S(2)}) collective-permute-start(bf16[512,512]{1,0:T(8,128)(2,1)} %get-tuple-element.34), channel_id=1, source_target_pairs={{1,2},{3,4},{5,6},{7,8},{9,10},{11,12},{13,14},{2,1},{4,3},{6,5},{... | collective-permute-start | bytes 1572872 | tf_op jit(solution)/shard_map/ppermute | solution.py:433
